TPU v7x, 32 devices: a whole 2x2x4 slice. The times are simulated.
32 devices in a mesh: groups: 2 (over y), det: 4 (over z), wafer: 2 (over x), rep: 2 (over core).
Axes of the slice: x: 2, y: 2, z: 4, core: 2. Of those that a mesh axis runs over, the one named last changes fastest.
Arguments:
- tod: float32 [4, 32, 4096], P(('groups', 'wafer'), 'det', 'rep'), parts along dimension 0, may hold values from -6 to 6
- psi: float32 [4, 32, 4096], P(('groups', 'wafer'), 'det', 'rep'), parts along dimension 0, may hold values from -3.140625 to 3.140625
- point_row: int32 [4, 32, 32], P(('groups', 'wafer'), 'det', 'rep'), parts along dimension 0, may hold values from 0 to 24575
- hit_list: int32 [4, 4, 2, 8, 32], P(('groups', 'wafer'), 'det', 'rep'), parts along dimension 0, may hold values from 0 to 128, as said below
- group_id: int32 [4, 32], P(('groups', 'wafer'), 'det'), parts along dimension 0, may hold values from 0 to 3, as said below
- a_zero: float32 [4, 32], P(('groups', 'wafer'), 'det'), parts along dimension 0, may hold values from 2 to 8
- band_coef: float32 [4, 32, 4], P(('groups', 'wafer'), 'det'), parts along dimension 0, may hold values from -0.2 to 0.2
- band_lag: int32 [4, 32, 4], P(('groups', 'wafer'), 'det'), parts along dimension 0, may hold values from 1 to 16
Outputs:
- solution: float32 [393216, 192], P(('groups', 'det', 'wafer')), parts along dimension 0
- residual: float32 [393216, 192], P(('groups', 'det', 'wafer')), parts along dimension 0
There are 2 independent parts, one for each index of `groups`. A program takes and returns all parts, laid end to end along the dimension named above; each array names one. Nothing has to cross between parts.
Inputs may be any that keep to these rules, and one draw needn't show every extreme that they name: `hit_list`: every sample block of a device (numbers 0 to 127) stands exactly once in that device's table; unused entries hold 128. In every draw some owner receives 32 blocks from every device. `group_id`: in every draw one readout group of some wafer has no detector.
All inputs are finite; a program needn't handle non-finite values.
Results may differ from a plain program's by a relative error of at most 0.0003.
Values sent between devices are 32-bit elements; how exact they have to be, the bound alone decides.
No kernel may reach another device: no remote copies, remote signals or barrier semaphores. Data moves between devices by JAX's collectives and lax.ppermute only.
A program may use at most 448 MiB of HBM per device.

v0:
```python
import jax
import jax.numpy as jnp
from jax import lax
from jax.sharding import PartitionSpec as P

BLOCKS = 196608
PBLOCK = 64
SBLOCK = 128
NSUB = 4
LAG = 16
ITERS = 3


prior_weight = 1.0


def with_halo(block, sides, width):
    for axis, dim in sides:
        count = lax.axis_size(axis)
        forward = [(i, i + 1) for i in range(count - 1)]
        backward = [(target, source) for source, target in forward]
        low = lax.ppermute(
            lax.slice_in_dim(block, block.shape[dim] - width, None, axis=dim), axis, forward
        )
        high = lax.ppermute(lax.slice_in_dim(block, 0, width, axis=dim), axis, backward)
        block = jnp.concatenate([low, block, high], axis=dim)
    return block


def local(tod, psi, point_row, hit_list, group_id, a_zero, band_coef, band_lag):
    highest = lax.Precision.HIGHEST
    samples = tod[0]
    angles = psi[0]
    det_count, time_count = samples.shape
    time_blocks = time_count // SBLOCK
    block_count = det_count * time_blocks
    send_table = hit_list[0, 0, 0]
    owner_count, capacity = send_table.shape
    owner_rows = BLOCKS // owner_count
    block_width = 3 * PBLOCK
    detector = lax.axis_index("det") * det_count + jnp.arange(det_count, dtype=jnp.int32)
    within = (jnp.arange(SBLOCK, dtype=jnp.int32)[None, :] + 3 * detector[:, None]) % PBLOCK
    pixel_table = (within[:, :, None] == jnp.arange(PBLOCK, dtype=jnp.int32)[None, None, :]).astype(
        jnp.float32
    )
    cosine_two = jnp.cos(2.0 * angles).reshape(det_count, time_blocks, SBLOCK)
    sine_two = jnp.sin(2.0 * angles).reshape(det_count, time_blocks, SBLOCK)
    slot_ids = send_table.reshape(-1)
    row_source = jnp.concatenate([point_row[0].reshape(-1), jnp.zeros((1,), jnp.int32)])
    slot_rows = row_source[slot_ids].astype(jnp.float32).reshape(owner_count, capacity)
    member = (group_id[0][:, None] == jnp.arange(NSUB, dtype=jnp.int32)[None, :]).astype(
        jnp.float32
    )
    member_count = jnp.sum(member, axis=0)
    lag_table = (
        band_lag[0][:, :, None] == jnp.arange(1, LAG + 1, dtype=jnp.int32)[None, None, :]
    ).astype(jnp.float32)
    lag_weight = jnp.einsum("dj,djl->dl", band_coef[0], lag_table, precision=highest)
    base_weight = a_zero[0]

    def slot_payload(by_block):
        width = by_block.shape[1]
        extended = jnp.concatenate([by_block, jnp.zeros((1, width), by_block.dtype)])
        return extended[slot_ids].reshape(owner_count, capacity, width)

    def deliver(payload):
        width = payload.shape[-1]
        got_values, got_rows = (
            lax.all_to_all(payload, ("det", "wafer"), split_axis=0, concat_axis=0, tiled=True),
            lax.all_to_all(slot_rows, ("det", "wafer"), split_axis=0, concat_axis=0, tiled=True),
        )
        return (got_values, got_rows)

    def back_project(stream, squared):
        shaped = stream.reshape(det_count, time_blocks, SBLOCK)
        first = cosine_two * cosine_two if squared else cosine_two
        second = sine_two * sine_two if squared else sine_two
        stacked = jnp.stack([shaped, first * shaped, second * shaped], axis=2)
        stokes = jnp.einsum("dkcs,dsp->dkcp", stacked, pixel_table, precision=highest)
        return stokes.reshape(block_count, block_width)

    def to_owners(stream, squared):
        got_values, got_rows = deliver(slot_payload(back_project(stream, squared)))
        pair_values, pair_rows = (
            lax.all_gather(got_values, "rep", axis=0, tiled=True),
            lax.all_gather(got_rows, "rep", axis=0, tiled=True),
        )
        target_rows = pair_rows.reshape(-1).astype(jnp.int32)
        summed = (
            jnp.zeros((owner_rows, block_width), jnp.float32)
            .at[target_rows]
            .add(pair_values.reshape(-1, block_width))
        )
        return (summed, got_rows.astype(jnp.int32))

    def remove_common(stream):
        local_sums = jnp.einsum("dg,dt->gt", member, stream, precision=highest)
        group_sums, group_counts = lax.psum((local_sums, member_count), "det")
        group_means = group_sums / jnp.maximum(group_counts, 1.0)[:, None]
        return stream - jnp.einsum("dg,gt->dt", member, group_means, precision=highest)

    def band_filter(stream):
        padded = with_halo(stream, (("rep", 1),), LAG)
        result = base_weight[:, None] * stream
        for offset in range(1, LAG + 1):
            later = padded[:, LAG + offset : LAG + offset + time_count]
            earlier = padded[:, LAG - offset : LAG - offset + time_count]
            result = result + lag_weight[:, offset - 1 : offset] * (later + earlier)
        return result

    def weigh_stream(stream):
        return remove_common(band_filter(remove_common(stream)))

    weight_stream = jnp.broadcast_to(base_weight[:, None], (det_count, time_count))
    diag_sum, serve_rows = to_owners(weight_stream, True)
    inverse_diag = 1.0 / (diag_sum + prior_weight)
    right_side = to_owners(weigh_stream(samples), False)[0]
    solution = jnp.zeros_like(right_side)
    residual = right_side

    def inner(left_map, right_map):
        return lax.psum(jnp.sum(left_map * right_map), ("det", "wafer"))

    precond = inverse_diag * residual
    direction = precond
    energy = inner(residual, precond)
    for iteration in range(ITERS):
        from_blocks = direction[serve_rows.reshape(-1)].reshape(owner_count, capacity, block_width)
        return_width = from_blocks.shape[-1]
        returned = lax.all_to_all(
            from_blocks, ("det", "wafer"), split_axis=0, concat_axis=0, tiled=True
        )
        return_placed = jnp.zeros((block_count + 1, return_width), jnp.float32)
        return_placed = return_placed.at[slot_ids].set(returned.reshape(-1, return_width))
        blocks = return_placed[:block_count].reshape(det_count, time_blocks, 3, PBLOCK)
        project_stokes = jnp.einsum("dkcp,dsp->dkcs", blocks, pixel_table, precision=highest)
        project_stream = (
            project_stokes[:, :, 0]
            + cosine_two * project_stokes[:, :, 1]
            + sine_two * project_stokes[:, :, 2]
        )
        seen_stream = project_stream.reshape(det_count, time_count)
        image_map = to_owners(weigh_stream(seen_stream), False)[0] + prior_weight * direction
        step_size = energy / inner(direction, image_map)
        solution = solution + step_size * direction
        residual = residual - step_size * image_map
        precond = inverse_diag * residual
        energy_next = inner(residual, precond)
        direction = precond + energy_next / energy * direction
        energy = energy_next
    return (solution, residual)


def solution(mesh):
    placed = (
        P(("groups", "wafer"), "det", "rep"),
        P(("groups", "wafer"), "det", "rep"),
        P(("groups", "wafer"), "det", "rep"),
        P(("groups", "wafer"), "det", "rep", None, None),
        P(("groups", "wafer"), "det"),
        P(("groups", "wafer"), "det"),
        P(("groups", "wafer"), "det", None),
        P(("groups", "wafer"), "det", None),
    )
    return jax.shard_map(
        local,
        mesh=mesh,
        in_specs=placed,
        out_specs=(P(("groups", "det", "wafer"), None), P(("groups", "det", "wafer"), None)),
        check_vma=False,
    )
```

profile of v0, /device:TPU:0, one launch (start us, length us, event | category | flops | bytes accessed | tf_op | source)
XLA Modules:
  0.0 873.0 jit_solution(13458776062378680690)
XLA Ops:
  13.9 19.8 %all-reduce.6 = (f32[4,2048]{1,0:T(4,128)S(1)}, f32[4]{0:T(128)S(1)}) all-reduce(f32[4,2048]{1,0:T(4,128)S(1)} %fusion.385, f32[4]{0:T(128)S(1)} %convert_reduce_fusion.2), channel_id=1, replica_groups=mesh['groups'=2,'det'=4,'wafer'=2,'rep'=2] {'det'}, use_global_device_ids=true, to_apply=%region_0.1 | all-reduce | flops 8196 | bytes 65568 | tf_op jit(solution)/shard_map/psum | solution.py:98
  115.3 25.7 %fusion.439 = f32[24576,192]{1,0:T(8,128)} fusion(f32[24576,192]{1,0:T(8,128)} %scatter_custom_fusion, f32[24576,192]{1,0:T(8,128)} %scatter_custom_fusion.1), kind=kLoop, calls=%fused_computation.746 | loop fusion | flops 9437184 | bytes 56623104 | tf_op jit(solution)/shard_map/mul | solution.py:124
  232.3 19.5 %scatter_fusion = f32[24576,192]{1,0:T(8,128)} fusion(f32[24576,192]{1,0:T(8,128)} %copy.245, s32[512]{0:T(512)S(1)} %bitcast.189, f32[512,192]{1,0:T(8,128)S(1)} %bitcast.160), kind=kCustom, calls=%fused_computation.12 | custom fusion | flops 98304 | bytes 1181696 | tf_op jit(solution)/shard_map/scatter-add | solution.py:92
  251.8 24.6 %multiply_reduce_fusion.4 = (f32[]{:T(128)}, f32[]{:T(128)}) fusion(f32[24576,192]{1,0:T(8,128)} %fusion.439, f32[24576,192]{1,0:T(8,128)} %scatter_fusion, f32[24576,192]{1,0:T(8,128)} %scatter_custom_fusion), kind=kLoop, calls=%fused_computation.27 | loop fusion | flops 18874366 | bytes 56623112 | tf_op jit(solution)/shard_map/reduce_sum | solution.py:122
  276.4 22.5 %all-reduce.5 = (f32[]{:T(128)}, f32[]{:T(128)}) all-reduce(f32[]{:T(128)} %get-tuple-element.13, f32[]{:T(128)} %get-tuple-element.12), channel_id=1, replica_groups=mesh['groups'=2,'det'=4,'wafer'=2,'rep'=2] {'det','wafer'}, use_global_device_ids=true, to_apply=%region_7.8 | all-reduce | flops 2 | bytes 16 | tf_op jit(solution)/shard_map/psum | solution.py:122
  300.2 33.9 %multiply_reduce_fusion.3 = (f32[]{:T(128)}, f32[24576,192]{1,0:T(8,128)}) fusion(f32[24576,192]{1,0:T(8,128)} %scatter_custom_fusion.1, f32[24576,192]{1,0:T(8,128)} %scatter_custom_fusion, f32[24576,192]{1,0:T(8,128)} %scatter_fusion, f32[]{:T(128)S(6)} %div.36), kind=kLoop, calls=%fused_computation.25 | loop fusion | flops 28311552 | bytes 75497480 | tf_op jit(solution)/shard_map/reduce_sum | solution.py:122
  334.0 17.8 %psum.133 = f32[]{:T(128)} all-reduce(f32[]{:T(128)} %get-tuple-element.20), channel_id=1, replica_groups=mesh['groups'=2,'det'=4,'wafer'=2,'rep'=2] {'det','wafer'}, use_global_device_ids=true, to_apply=%region_15.16 | all-reduce | flops 1 | bytes 8 | tf_op jit(solution)/shard_map/psum | solution.py:122
  353.0 32.9 %multiply_add_fusion.2 = f32[24576,192]{1,0:T(8,128)} fusion(f32[24576,192]{1,0:T(8,128)} %fusion.439, f32[]{:T(128)S(6)} %div.37, f32[24576,192]{1,0:T(8,128)} %get-tuple-element.21, f32[24576,192]{1,0:T(8,128)} %scatter_custom_fusion.1), kind=kLoop, calls=%fused_computation.24 | loop fusion | flops 18874368 | bytes 75497472 | tf_op jit(solution)/shard_map/add | solution.py:149
  431.3 17.1 %psum.135 = f32[4,2048]{1,0:T(4,128)S(1)} all-reduce(f32[4,2048]{1,0:T(4,128)S(1)} %fusion.411), channel_id=1, replica_groups=mesh['groups'=2,'det'=4,'wafer'=2,'rep'=2] {'det'}, use_global_device_ids=true, to_apply=%region_18.19 | all-reduce | flops 8192 | bytes 65536 | tf_op jit(solution)/shard_map/psum | solution.py:98
  473.7 19.5 %scatter_fusion.1 = f32[24576,192]{1,0:T(8,128)} fusion(f32[24576,192]{1,0:T(8,128)} %copy.246, s32[512]{0:T(512)S(1)} %bitcast.190, f32[512,192]{1,0:T(8,128)S(1)} %bitcast.161), kind=kCustom, calls=%fused_computation.14 | custom fusion | flops 98304 | bytes 1181696 | tf_op jit(solution)/shard_map/scatter-add | solution.py:92
  493.1 17.3 %multiply_reduce_fusion.2 = f32[]{:T(128)} fusion(f32[24576,192]{1,0:T(8,128)} %multiply_add_fusion.2, f32[24576,192]{1,0:T(8,128)} %scatter_fusion.1), kind=kLoop, calls=%fused_computation.23 | loop fusion | flops 9437183 | bytes 37748740 | tf_op jit(solution)/shard_map/reduce_sum | solution.py:122
  510.4 22.4 %psum.136 = f32[]{:T(128)} all-reduce(f32[]{:T(128)} %multiply_reduce_fusion.2), channel_id=1, replica_groups=mesh['groups'=2,'det'=4,'wafer'=2,'rep'=2] {'det','wafer'}, use_global_device_ids=true, to_apply=%region_21.22 | all-reduce | flops 1 | bytes 8 | tf_op jit(solution)/shard_map/psum | solution.py:122
  534.1 33.8 %multiply_reduce_fusion.1 = (f32[]{:T(128)}, f32[24576,192]{1,0:T(8,128)}) fusion(f32[24576,192]{1,0:T(8,128)} %scatter_custom_fusion.1, f32[24576,192]{1,0:T(8,128)} %get-tuple-element.21, f32[24576,192]{1,0:T(8,128)} %scatter_fusion.1, f32[]{:T(128)S(6)} %div.78), kind=kLoop, calls=%fused_computation.21 | loop fusion | flops 28311552 | bytes 75497480 | tf_op jit(solution)/shard_map/reduce_sum | solution.py:122
  567.9 17.7 %psum.137 = f32[]{:T(128)} all-reduce(f32[]{:T(128)} %get-tuple-element.18), channel_id=1, replica_groups=mesh['groups'=2,'det'=4,'wafer'=2,'rep'=2] {'det','wafer'}, use_global_device_ids=true, to_apply=%region_23.24 | all-reduce | flops 1 | bytes 8 | tf_op jit(solution)/shard_map/psum | solution.py:122
  586.9 33.0 %multiply_add_fusion.1 = f32[24576,192]{1,0:T(8,128)} fusion(f32[24576,192]{1,0:T(8,128)} %multiply_add_fusion.2, f32[]{:T(128)S(6)} %div.79, f32[24576,192]{1,0:T(8,128)} %get-tuple-element.19, f32[24576,192]{1,0:T(8,128)} %scatter_custom_fusion.1), kind=kLoop, calls=%fused_computation.20 | loop fusion | flops 18874368 | bytes 75497472 | tf_op jit(solution)/shard_map/add | solution.py:149
  665.3 17.1 %psum.139 = f32[4,2048]{1,0:T(4,128)S(1)} all-reduce(f32[4,2048]{1,0:T(4,128)S(1)} %fusion.409), channel_id=1, replica_groups=mesh['groups'=2,'det'=4,'wafer'=2,'rep'=2] {'det'}, use_global_device_ids=true, to_apply=%region_26.27 | all-reduce | flops 8192 | bytes 65536 | tf_op jit(solution)/shard_map/psum | solution.py:98
  688.4 16.8 %copy.247 = f32[24576,192]{1,0:T(8,128)} copy(f32[24576,192]{1,0:T(8,128)} %multiply_add_fusion.1) | data formatting | bytes 37748736
  707.7 19.5 %scatter_fusion.2 = f32[24576,192]{1,0:T(8,128)} fusion(f32[24576,192]{1,0:T(8,128)} %copy.247, s32[512]{0:T(512)S(1)} %bitcast.191, f32[512,192]{1,0:T(8,128)S(1)} %bitcast.159), kind=kCustom, calls=%fused_computation.16 | custom fusion | flops 98304 | bytes 1181696 | tf_op jit(solution)/shard_map/scatter-add | solution.py:92
  727.2 17.3 %multiply_reduce_fusion = f32[]{:T(128)} fusion(f32[24576,192]{1,0:T(8,128)} %multiply_add_fusion.1, f32[24576,192]{1,0:T(8,128)} %scatter_fusion.2), kind=kLoop, calls=%fused_computation.19 | loop fusion | flops 9437183 | bytes 37748740 | tf_op jit(solution)/shard_map/reduce_sum | solution.py:122
  744.5 22.4 %psum.140 = f32[]{:T(128)} all-reduce(f32[]{:T(128)} %multiply_reduce_fusion), channel_id=1, replica_groups=mesh['groups'=2,'det'=4,'wafer'=2,'rep'=2] {'det','wafer'}, use_global_device_ids=true, to_apply=%region_29.30 | all-reduce | flops 1 | bytes 8 | tf_op jit(solution)/shard_map/psum | solution.py:122
  768.2 33.0 %multiply_add_fusion = f32[24576,192]{1,0:T(8,128)} fusion(f32[24576,192]{1,0:T(8,128)} %multiply_add_fusion.1, f32[24576,192]{1,0:T(8,128)} %multiply_add_fusion.2, f32[24576,192]{1,0:T(8,128)} %fusion.439, f32[]{:T(128)S(6)} %div.82, f32[]{:T(128)S(6)} %div.78, f32[]{:T(128)S(6)} %div.36), kind=kLoop, calls=%fused_computation.18 | loop fusion | flops 23592960 | bytes 75497488 | tf_op jit(solution)/shard_map/add | solution.py:145
  801.2 25.6 %multiply_subtract_fusion = f32[24576,192]{1,0:T(8,128)} fusion(f32[24576,192]{1,0:T(8,128)} %get-tuple-element.19, f32[24576,192]{1,0:T(8,128)} %scatter_fusion.2, f32[]{:T(128)S(6)} %div.82), kind=kLoop, calls=%fused_computation.17 | loop fusion | flops 9437184 | bytes 56623108 | tf_op jit(solution)/shard_map/sub | solution.py:146
  826.8 22.9 %copy.176 = f32[24576,192]{0,1:T(8,128)} copy(f32[24576,192]{1,0:T(8,128)} %multiply_subtract_fusion) | data formatting | bytes 37748736
  849.7 22.9 %copy.175 = f32[24576,192]{0,1:T(8,128)} copy(f32[24576,192]{1,0:T(8,128)} %multiply_add_fusion) | data formatting | bytes 37748736
  (168 shorter events, 309.9 us)
Async XLA Ops:
  4.8 63.5 %all-to-all-start = ((f32[8,1,32]{2,1,0:T(1,128)}), f32[8,1,32]{2,1,0:T(1,128)S(1)}, u32[]{:S(2)}, u32[]{:S(2)}) async-start(f32[8,1,32]{2,1,0:T(1,128)} %convert_element_type.51), calls=%async_computation | async-start | bytes 8192 | tf_op jit(solution)/shard_map/all_to_all | solution.py:70
  34.9 8.5 collective-permute-start
  36.2 7.2 collective-permute-start.1
  68.4 12.2 %all-to-all-start.1 = ((f32[8,32,192]{2,1,0:T(8,128)}), f32[8,32,192]{2,1,0:T(8,128)S(1)}, u32[]{:S(2)}, u32[]{:S(2)}) async-start(f32[8,32,192]{2,1,0:T(8,128)} %bitcast.28), calls=%async_computation.1 | async-start | bytes 524288 | tf_op jit(solution)/shard_map/all_to_all | solution.py:69
  80.6 18.9 %all-to-all-start.2 = ((f32[8,32,192]{2,1,0:T(8,128)}), f32[8,32,192]{2,1,0:T(8,128)S(1)}, u32[]{:S(2)}, u32[]{:S(2)}) async-start(f32[8,32,192]{2,1,0:T(8,128)} %bitcast.31), calls=%async_computation.2 | async-start | bytes 524288 | tf_op jit(solution)/shard_map/all_to_all | solution.py:69
  115.3 51.7 %copy-start = (f32[1,8,2048]{2,1,0:T(8,128)S(1)}, f32[1,8,2048]{2,1,0:T(8,128)}, u32[]{:S(2)}) copy-start(f32[1,8,2048]{2,1,0:T(8,128)} %param.9) | copy-start | bytes 196612
  115.3 51.9 %copy-start.1 = (s32[1,8]{1,0:T(1,128)S(1)}, s32[1,8]{1,0:T(1,128)}, u32[]{:S(2)}) copy-start(s32[1,8]{1,0:T(1,128)} %param.12) | copy-start | bytes 100
  115.3 74.4 %copy-start.2 = (f32[1,8]{1,0:T(1,128)S(1)}, f32[1,8]{1,0:T(1,128)}, u32[]{:S(2)}) copy-start(f32[1,8]{1,0:T(1,128)} %param.13) | copy-start | bytes 100
  184.5 4.3 collective-permute-start.2
  185.8 3.8 collective-permute-start.3
  209.6 20.4 %all-to-all-start.4 = ((f32[8,32,192]{2,1,0:T(8,128)}), f32[8,32,192]{2,1,0:T(8,128)S(1)}, u32[]{:S(2)}, u32[]{:S(2)}) async-start(f32[8,32,192]{2,1,0:T(8,128)} %bitcast.39), calls=%async_computation.4 | async-start | bytes 524288 | tf_op jit(solution)/shard_map/all_to_all | solution.py:69
  425.4 4.3 collective-permute-start.4
  426.7 3.8 collective-permute-start.5
  451.1 20.2 %all-to-all-start.6 = ((f32[8,32,192]{2,1,0:T(8,128)}), f32[8,32,192]{2,1,0:T(8,128)S(1)}, u32[]{:S(2)}, u32[]{:S(2)}) async-start(f32[8,32,192]{2,1,0:T(8,128)} %bitcast.44), calls=%async_computation.6 | async-start | bytes 524288 | tf_op jit(solution)/shard_map/all_to_all | solution.py:69
  659.3 4.3 collective-permute-start.6
  660.6 3.8 collective-permute-start.7
  685.0 20.3 %all-to-all-start.8 = ((f32[8,32,192]{2,1,0:T(8,128)}), f32[8,32,192]{2,1,0:T(8,128)S(1)}, u32[]{:S(2)}, u32[]{:S(2)}) async-start(f32[8,32,192]{2,1,0:T(8,128)} %bitcast.49), calls=%async_computation.8 | async-start | bytes 524288 | tf_op jit(solution)/shard_map/all_to_all | solution.py:69
where the time goes:
time: 883 us; the launch traced here: 873 us
  other arithmetic  369 us (42%)
  blocking collectives  290 us (33%)
  local copies, waits for them, and re-layouts  146 us (17%)
  starting transfers between devices  42.4 us (5%)
    psum x8, blocking collectives, remove_common(): group_sums, group_counts = lax.psum((local_sums, member_count), 'det')  136 us
    reduce_sum x5, other arithmetic, inner(): return lax.psum(jnp.sum(left_map * right_map), ('det', 'wafer'))  127 us
    psum x5, blocking collectives, inner(): return lax.psum(jnp.sum(left_map * right_map), ('det', 'wafer'))  103 us
    unnamed x31, local copies, waits for them, and re-layouts  98.3 us
    scatter-add x5, other arithmetic, to_owners(): summed = jnp.zeros((owner_rows, block_width), jnp.float32).at[target_rows...  84.8 us
    add x2, other arithmetic, local(): direction = precond + energy_next / energy * direction  65.9 us
    all_to_all x3, blocking collectives, local(): lax.all_to_all(from_blocks, ('det', 'wafer'), split_axis=0, concat_axis=0...  37.9 us
    add x1, other arithmetic, local(): solution = solution + step_size * direction  33 us
  transfers between devices with their start and end apart: 14, of which 4 were waited for; matrix products, arithmetic and copies ran while one was open for 9% of the time, Pallas kernels for 0%

commit v1 on v0

--- a/solution.py
+++ b/solution.py
@@ -1,6 +1,10 @@
+import functools
+
 import jax
 import jax.numpy as jnp
 from jax import lax
+from jax.experimental import pallas as pl
+from jax.experimental.pallas import tpu as pltpu
 from jax.sharding import PartitionSpec as P
 
 BLOCKS = 196608
@@ -27,7 +31,7 @@
     return block
 
 
-def local(tod, psi, point_row, hit_list, group_id, a_zero, band_coef, band_lag):
+def distributed(tod, psi, point_row, hit_list, group_id, a_zero, band_coef, band_lag):
     highest = lax.Precision.HIGHEST
     samples = tod[0]
     angles = psi[0]
@@ -151,6 +155,552 @@
     return (solution, residual)
 
 
+LANES = 128
+ROWS = 8
+OUT_TILES = 4
+BIG = float(1 << 24)
+VMEM_BYTES = 60 << 20
+
+
+def lane_take(block, index):
+    return jnp.take_along_axis(block, index, axis=1, mode="promise_in_bounds")
+
+
+def cosine_sine_double(angle):
+    turns = jnp.floor(angle * 1.2732395447351628 + 0.5)
+    reduced = 2.0 * angle - turns * 1.5703125
+    reduced = reduced - turns * 4.837512969970703125e-4
+    reduced = reduced - turns * 7.54978995489188216e-8
+    square = reduced * reduced
+    sine = (-1.9515295891e-4 * square + 8.3321608736e-3) * square - 1.6666654611e-1
+    sine = sine * square * reduced + reduced
+    cosine = (2.443315711809948e-5 * square - 1.388731625493765e-3) * square
+    cosine = (cosine + 4.166664568298827e-2) * square * square - 0.5 * square + 1.0
+    quarter = turns.astype(jnp.int32)
+    odd = (quarter & 1) == 1
+    first = jnp.where(odd, sine, cosine)
+    second = jnp.where(odd, cosine, sine)
+    first = jnp.where(((quarter + 1) & 2) == 2, -first, first)
+    second = jnp.where((quarter & 2) == 2, -second, second)
+    return first, second
+
+
+def whole_part_kernel(
+    shape, own_ref, part_ref, x_ref, r_ref,
+    cos_ref, sin_ref, clean_ref, inverse_ref, x_map, r_map, d_map, image_map, weight_ref,
+    member_ref, share_ref, base_ref, coef_ref, lag_ref, high_ref, low_ref, place_ref, full_ref,
+    code_ref, table_ref, start_ref, rows_ref, sorted_ref, column_ref, x_buffer, r_buffer,
+    table_smem, start_smem, twin_smem, table_sem, x_sem, r_sem,
+):
+    wafers, dets, reps, tiles, owners, capacity, owner_rows, lag_count = shape
+    teams = wafers * dets
+    devices = teams * reps
+    blocks = reps * tiles
+    total = devices * tiles * ROWS
+    span = tiles * LANES
+    params = 2 * span
+    extra = params + LANES
+    groups = owner_rows // LANES
+    lane = lax.broadcasted_iota(jnp.int32, (ROWS, LANES), 1)
+    sub = lax.broadcasted_iota(jnp.int32, (ROWS, LANES), 0)
+    lane_f = lane.astype(jnp.float32)
+    own = own_ref[0]
+    first_row = (own * owner_rows).astype(jnp.float32)
+
+    def wide(column):
+        return jnp.broadcast_to(column, (ROWS, LANES))
+
+    def fold(block):
+        return block + pltpu.roll(block, LANES // 2, 1)
+
+    for team in range(teams):
+        values = part_ref[team * reps, :, params : params + LANES]
+        base_ref[team] = wide(values[:, tiles + 1 : tiles + 2])
+        for group in range(NSUB):
+            member_ref[team, group] = wide(
+                (values[:, tiles : tiles + 1] == float(group)).astype(jnp.float32)
+            )
+        for j in range(lag_count):
+            at = tiles + 2 + j
+            coef_ref[team, j] = wide(values[:, at : at + 1])
+            lag_ref[team, j] = wide(values[:, at + lag_count : at + lag_count + 1].astype(jnp.int32))
+        clean_ref[team, 0] = jnp.zeros((ROWS, LANES), jnp.float32)
+        clean_ref[team, blocks + 1] = jnp.zeros((ROWS, LANES), jnp.float32)
+    for wafer in range(wafers):
+        for group in range(NSUB):
+            count = member_ref[wafer * dets, group]
+            for i in range(1, dets):
+                count = count + member_ref[wafer * dets + i, group]
+            count = jnp.sum(count, axis=0, keepdims=True)
+            share_ref[wafer, group] = wide(1.0 / jnp.maximum(count, 1.0))
+
+    def survey(device, carry):
+        team = device // reps
+        values = part_ref[device, :, params : params + LANES]
+        base = base_ref[team]
+        codes = jnp.full((ROWS, LANES), BIG, jnp.float32)
+        for b in range(tiles):
+            at = device * tiles + b
+            first, second = cosine_sine_double(part_ref[device, :, b * LANES : (b + 1) * LANES])
+            cos_ref[at] = first
+            sin_ref[at] = second
+            image_map[at, 0] = base + base
+            image_map[at, 1] = fold(base * (first * first))
+            image_map[at, 2] = fold(base * (second * second))
+            ids = wide(values[:, b : b + 1])
+            least = jnp.full((ROWS, LANES), BIG, jnp.float32)
+            for other in range(devices):
+                row = part_ref[other, 0:1, extra : extra + LANES]
+                least = jnp.minimum(least, jnp.where(ids == row, lane_f + float(other * LANES), BIG))
+            least = jnp.min(least, axis=1, keepdims=True)
+            mine = (device * LANES + sub[:, 0:1] * tiles + b).astype(jnp.float32)
+            weight_ref[at] = wide(jnp.where(least == mine, 0.5, 0.0))
+            code = jnp.where(least < mine, mine * float(total) + least, BIG)
+            codes = jnp.where(lane == b, code, codes)
+            local_row = ids - first_row
+            high = jnp.floor(local_row * (1.0 / LANES))
+            low = local_row - high * LANES
+            at_row = pl.ds(pl.multiple_of(at * ROWS, ROWS), ROWS)
+            high_ref[at_row, 0:LANES] = (high == lane_f).astype(jnp.float32)
+            high_ref[at_row, LANES : 2 * LANES] = (high == lane_f + LANES).astype(jnp.float32)
+            low_ref[at_row, :] = (low == lane_f).astype(jnp.float32)
+        code_ref[device] = codes
+        return carry
+
+    lax.fori_loop(0, devices, survey, 0)
+
+    def exact_dot(left, right, dims):
+        return lax.dot_general(
+            left.astype(jnp.bfloat16), right.astype(jnp.bfloat16), (dims, ((), ())),
+            preferred_element_type=jnp.float32,
+        )
+
+    depth = 2 * LANES
+    hits = exact_dot(high_ref[...], low_ref[...], ((0,), (0,)))
+    full = jnp.minimum(hits, 1.0)
+    full_ref[...] = full
+    before = (
+        lax.broadcasted_iota(jnp.int32, (LANES, LANES), 0)
+        < lax.broadcasted_iota(jnp.int32, (LANES, LANES), 1)
+    ).astype(jnp.float32)
+    above = (
+        lax.broadcasted_iota(jnp.int32, (depth, depth), 1)
+        < lax.broadcasted_iota(jnp.int32, (depth, depth), 0)
+    ).astype(jnp.float32)
+    in_tile = exact_dot(full, before, ((1,), (0,)))
+    tile_sum = exact_dot(full, jnp.ones((LANES, LANES), jnp.float32), ((1,), (0,)))
+    start = exact_dot(above, tile_sum, ((1,), (0,)))
+    place = in_tile + start
+    place_ref[...] = place.astype(jnp.int32)
+    start_ref[...] = start.astype(jnp.int32)
+    place_high = jnp.floor(place * (1.0 / LANES))
+    place_low = place - place_high * LANES
+
+    def rank_of(device, carry):
+        at_rows = pl.ds(pl.multiple_of(device * LANES, LANES), LANES)
+        high = high_ref[at_rows, :]
+        rank = LANES * exact_dot(high, place_high, ((1,), (0,))) + exact_dot(
+            high, place_low, ((1,), (0,))
+        )
+        rank = jnp.sum(rank * low_ref[at_rows, :], axis=1, keepdims=True)
+        table = jnp.zeros((ROWS, LANES), jnp.float32)
+        for b in range(tiles):
+            table = jnp.where(lane == b, rank[b * ROWS : (b + 1) * ROWS], table)
+        table_ref[device, 0:ROWS] = table.astype(jnp.int32)
+        table_ref[device, ROWS : 2 * ROWS] = part_ref[device, :, extra : extra + LANES].astype(
+            jnp.int32
+        )
+        return carry
+
+    lax.fori_loop(0, devices, rank_of, 0)
+    copies = (
+        pltpu.make_async_copy(table_ref, table_smem, table_sem.at[0]),
+        pltpu.make_async_copy(start_ref, start_smem, table_sem.at[1]),
+    )
+    for copy in copies:
+        copy.start()
+    for copy in copies:
+        copy.wait()
+
+    def next_code(last):
+        found = jnp.full((ROWS, LANES), BIG, jnp.float32)
+        for device in range(devices):
+            codes = code_ref[device]
+            found = jnp.minimum(found, jnp.where(codes > last, codes, BIG))
+        return jnp.min(found)
+
+    def take_twin(state):
+        count, code = state
+        twin_smem[count] = code.astype(jnp.int32)
+        return count + 1, next_code(code)
+
+    twin_count, _ = lax.while_loop(
+        lambda state: state[1] < BIG, take_twin, (jnp.int32(0), next_code(jnp.float32(-1.0)))
+    )
+
+    def locate(number):
+        device = lax.div(number, LANES)
+        inside = lax.rem(number, LANES)
+        row = lax.div(inside, tiles)
+        detector = lax.rem(lax.div(device, reps), dets) * ROWS + row
+        return device * tiles + lax.rem(inside, tiles), row, detector
+
+    def merge_twins(target):
+        def gather_one(n, carry):
+            code = twin_smem[n]
+            at, row, detector = locate(lax.div(code, total))
+            lead_at, lead_row, lead_detector = locate(lax.rem(code, total))
+            shift = (3 * (detector - lead_detector)) & (PBLOCK - 1)
+            for c in range(3):
+                moved = pltpu.roll(wide(target[at, c, pl.ds(row, 1), :]), shift, 1)
+                target[lead_at, c, pl.ds(lead_row, 1), :] += moved[0:1]
+            return carry
+
+        def spread_one(n, carry):
+            code = twin_smem[n]
+            at, row, detector = locate(lax.div(code, total))
+            lead_at, lead_row, lead_detector = locate(lax.rem(code, total))
+            shift = (3 * (lead_detector - detector)) & (PBLOCK - 1)
+            for c in range(3):
+                moved = pltpu.roll(wide(target[lead_at, c, pl.ds(lead_row, 1), :]), shift, 1)
+                target[at, c, pl.ds(row, 1), :] = moved[0:1]
+            return carry
+
+        lax.fori_loop(0, twin_count, gather_one, 0)
+        lax.fori_loop(0, twin_count, spread_one, 0)
+
+    def remove_common(wafer, streams):
+        means = []
+        for group in range(NSUB):
+            part = member_ref[wafer * dets, group] * streams[0]
+            for i in range(1, dets):
+                part = part + member_ref[wafer * dets + i, group] * streams[i]
+            means.append(jnp.sum(part, axis=0, keepdims=True) * share_ref[wafer, group])
+        result = []
+        for i in range(dets):
+            stream = streams[i]
+            for group in range(NSUB):
+                stream = stream - member_ref[wafer * dets + i, group] * means[group]
+            result.append(stream)
+        return result
+
+    def loop(count, body, carry, unroll):
+        def several(n, carry):
+            for k in range(unroll):
+                carry = body(n * unroll + k, carry)
+            return carry
+
+        return lax.fori_loop(0, count // unroll, several, carry)
+
+    def first_removal(stream_of, carry):
+        for wafer in range(wafers):
+
+            def one_time(block, carry):
+                streams = []
+                for i in range(dets):
+                    stream, carry = stream_of(wafer * dets + i, block, carry)
+                    streams.append(stream)
+                for i, stream in enumerate(remove_common(wafer, streams)):
+                    clean_ref[wafer * dets + i, block + 1] = stream
+                return carry
+
+            carry = loop(blocks, one_time, carry, 2)
+        return carry
+
+    def filter_and_return(target):
+        carry = jnp.zeros((ROWS, LANES), jnp.float32)
+        for wafer in range(wafers):
+
+            def one_time(block, carry):
+                streams = []
+                for i in range(dets):
+                    team = wafer * dets + i
+                    here = clean_ref[team, block + 1]
+                    after = clean_ref[team, block + 2]
+                    ahead = clean_ref[team, block]
+                    result = base_ref[team] * here
+                    for j in range(lag_count):
+                        lag = lag_ref[team, j]
+                        later = lane_take(
+                            jnp.where(lane < lag, after, here), (lane + lag) & (LANES - 1)
+                        )
+                        earlier = lane_take(
+                            jnp.where(lane >= LANES - lag, ahead, here), (lane - lag) & (LANES - 1)
+                        )
+                        result = result + coef_ref[team, j] * (later + earlier)
+                    carry = carry + here * result
+                    streams.append(result)
+                for i, stream in enumerate(remove_common(wafer, streams)):
+                    at = (wafer * dets + i) * blocks + block
+                    target[at, 0] = fold(stream)
+                    target[at, 1] = fold(cos_ref[at] * stream)
+                    target[at, 2] = fold(sin_ref[at] * stream)
+                return carry
+
+            carry = loop(blocks, one_time, carry, 2)
+        return carry
+
+    def whole_sum(values):
+        values = jnp.sum(values, axis=0, keepdims=True)
+        return wide(jnp.sum(values, axis=1, keepdims=True))
+
+    zero = jnp.zeros((ROWS, LANES), jnp.float32)
+    count = teams * blocks
+
+    merge_twins(image_map)
+
+    def data_stream(team, block, carry):
+        device = team * reps + lax.div(block, tiles)
+        at = pl.multiple_of(span + lax.rem(block, tiles) * LANES, LANES)
+        return part_ref[device, :, pl.ds(at, LANES)], carry
+
+    first_removal(data_stream, 0)
+    filter_and_return(r_map)
+    merge_twins(r_map)
+
+    def begin(at, carry):
+        parts = zero
+        for c in range(3):
+            inverse = 1.0 / (image_map[at, c] + prior_weight)
+            inverse_ref[at, c] = inverse
+            residual = r_map[at, c]
+            parts = parts + residual * (inverse * residual)
+        return carry + weight_ref[at] * parts
+
+    energy = whole_sum(loop(count, begin, zero, 2))
+    factor = zero
+    for iteration in range(ITERS):
+        last = iteration == ITERS - 1
+
+        def seen_stream(team, block, carry):
+            at = team * blocks + block
+            parts = []
+            for c in range(3):
+                part = inverse_ref[at, c] * r_map[at, c]
+                if iteration:
+                    part = part + factor * d_map[at, c]
+                d_map[at, c] = part
+                parts.append(part)
+            squares = parts[0] * parts[0] + parts[1] * parts[1] + parts[2] * parts[2]
+            stream = parts[0] + cos_ref[at] * parts[1] + sin_ref[at] * parts[2]
+            return stream, carry + weight_ref[at] * squares
+
+        prior = first_removal(seen_stream, zero)
+        product = filter_and_return(image_map)
+        merge_twins(image_map)
+        step = energy / whole_sum(product + prior_weight * prior)
+
+        def advance(at):
+            new_x, new_r = [], []
+            for c in range(3):
+                direction = d_map[at, c]
+                image = image_map[at, c] + prior_weight * direction
+                move = step * direction
+                new_x.append(x_map[at, c] + move if iteration else move)
+                new_r.append(r_map[at, c] - step * image)
+            return new_x, new_r
+
+        if not last:
+
+            def update(at, carry):
+                new_x, new_r = advance(at)
+                parts = zero
+                for c in range(3):
+                    x_map[at, c] = new_x[c]
+                    r_map[at, c] = new_r[c]
+                    parts = parts + new_r[c] * (inverse_ref[at, c] * new_r[c])
+                return carry + weight_ref[at] * parts
+
+            next_energy = whole_sum(loop(count, update, zero, 2))
+            factor = next_energy / energy
+            energy = next_energy
+        else:
+
+            def place_pixels(at, carry):
+                new_x, new_r = advance(at)
+                team = lax.rem(lax.div(at, blocks), dets)
+                turn = (lane - 3 * (team * ROWS + sub)) & (LANES - 1)
+                values = [lane_take(value, turn) for value in new_x + new_r]
+                rows = pl.ds(pl.multiple_of(at * ROWS, ROWS), ROWS)
+                for c in range(3):
+                    rows_ref[rows, c * LANES : (c + 1) * LANES] = jnp.where(
+                        lane < PBLOCK, values[2 * c], values[2 * c + 1]
+                    )
+                return carry
+
+            loop(count, place_pixels, 0, 2)
+
+    slots = devices * capacity
+    flat = own * capacity
+    hit_row = ROWS + 1 + lax.div(flat, LANES)
+    hit_lane = lax.rem(flat, LANES)
+
+    def pick(device, carry):
+        for c in range(capacity):
+            number = table_smem[device, hit_row, hit_lane + c]
+            valid = number < LANES
+            number = jnp.where(valid, number, 0)
+            row = lax.div(number, tiles)
+            column = lax.rem(number, tiles)
+            source = (device * tiles + column) * ROWS + row
+            target = jnp.where(valid, table_smem[device, row, column], slots)
+            sorted_ref[pl.ds(target, 1), :] = rows_ref[pl.ds(source, 1), :]
+        return carry
+
+    lax.fori_loop(0, devices, pick, 0)
+    for tile in range(slots // LANES):
+        column_ref[tile] = sorted_ref[tile * LANES : (tile + 1) * LANES, :].T
+
+    height = 3 * PBLOCK
+    step_width = OUT_TILES * LANES
+
+    def store_copies(n, slot):
+        to = pl.ds(pl.multiple_of(n * step_width, step_width), step_width)
+        return (
+            pltpu.make_async_copy(x_buffer.at[slot], x_ref.at[:, to], x_sem.at[slot]),
+            pltpu.make_async_copy(r_buffer.at[slot], r_ref.at[:, to], r_sem.at[slot]),
+        )
+
+    def write(n, carry):
+        slot = lax.rem(n, 2)
+
+        @pl.when(n >= 2)
+        def _():
+            for copy in store_copies(n - 2, slot):
+                copy.wait()
+
+        for k in range(OUT_TILES):
+            group = n * OUT_TILES + k
+            tile = lax.div(start_smem[group, 0], LANES)
+            index = wide(place_ref[pl.ds(group, 1), :]) & (LANES - 1)
+            split = wide(start_ref[pl.ds(group, 1), :]) & (LANES - 1)
+            present = wide(full_ref[pl.ds(group, 1), :]) > 0.0
+            follow = lane < split
+            for s in range(height // ROWS):
+                for buffer, offset in ((x_buffer, 0), (r_buffer, height)):
+                    rows = slice(offset + s * ROWS, offset + (s + 1) * ROWS)
+                    window = jnp.where(follow, column_ref[tile + 1, rows, :], column_ref[tile, rows, :])
+                    buffer[slot, s * ROWS : (s + 1) * ROWS, k * LANES : (k + 1) * LANES] = jnp.where(
+                        present, lane_take(window, index), 0.0
+                    )
+        for copy in store_copies(n, slot):
+            copy.start()
+        return carry
+
+    steps = groups // OUT_TILES
+    lax.fori_loop(0, steps, write, 0)
+    for n in (steps - 2, steps - 1):
+        for copy in store_copies(n, n % 2):
+            copy.wait()
+
+
+def part_shape(sizes, tod, hit_list, band_lag):
+    det_count, time_count = tod.shape[1:]
+    owners, capacity = hit_list.shape[3:]
+    return (
+        sizes["wafer"], sizes["det"], sizes["rep"], time_count // SBLOCK,
+        owners, capacity, BLOCKS // owners, band_lag.shape[2],
+    ), det_count
+
+
+def fits_one_device(shape, det_count):
+    wafers, dets, reps, tiles, owners, capacity, owner_rows, lag_count = shape
+    devices = wafers * dets * reps
+    total = devices * tiles * det_count
+    table_rows = owners * capacity // LANES
+    groups = owner_rows // LANES
+    return (
+        det_count == ROWS
+        and tiles * ROWS == LANES
+        and tiles + 2 + 2 * lag_count <= LANES
+        and reps * tiles % 2 == 0
+        and owners * capacity % LANES == 0
+        and LANES % capacity == 0
+        and table_rows < ROWS
+        and devices * capacity % LANES == 0
+        and owner_rows % (LANES * OUT_TILES) == 0
+        and 2 * OUT_TILES <= groups <= 2 * LANES
+        and total * total < BIG
+    )
+
+
+def whole_part(shape, tod, psi, point_row, hit_list, group_id, a_zero, band_coef, band_lag):
+    wafers, dets, reps, tiles, owners, capacity, owner_rows, lag_count = shape
+    teams = wafers * dets
+    devices = teams * reps
+    blocks = reps * tiles
+    count = devices * tiles
+    total = count * ROWS
+    slots = devices * capacity
+    table = hit_list[0, 0, 0]
+    found = table[:, :, None] == jnp.arange(LANES, dtype=jnp.int32)[None, None, :]
+    owner = jnp.arange(owners, dtype=jnp.int32)[:, None, None]
+    owner_of = jnp.sum(jnp.where(found, owner, 0), axis=(0, 1)).reshape(ROWS, tiles)
+    ids = (owner_of * owner_rows + point_row[0]).astype(jnp.float32)
+    per_detector = jnp.concatenate(
+        [
+            ids, group_id[0][:, None].astype(jnp.float32), a_zero[0][:, None], band_coef[0],
+            band_lag[0].astype(jnp.float32),
+        ],
+        axis=1,
+    )
+    per_detector = jnp.pad(per_detector, ((0, 0), (0, LANES - per_detector.shape[1])))
+    tables = jnp.concatenate([ids.reshape(-1), table.reshape(-1).astype(jnp.float32)])
+    tables = jnp.pad(tables, (0, ROWS * LANES - tables.shape[0])).reshape(ROWS, LANES)
+    payload = jnp.concatenate([psi[0], tod[0], per_detector, tables], axis=1)
+    gathered = lax.all_gather(payload, ("wafer", "det", "rep"), axis=0, tiled=False)
+    own = (lax.axis_index("det") * wafers + lax.axis_index("wafer")).astype(jnp.int32).reshape(1)
+
+    height = 3 * PBLOCK
+    f32 = jnp.float32
+    stream = pltpu.VMEM((count, ROWS, LANES), f32)
+    sky = pltpu.VMEM((count, 3, ROWS, LANES), f32)
+    x_turned, r_turned = pl.pallas_call(
+        functools.partial(whole_part_kernel, shape),
+        out_shape=[jax.ShapeDtypeStruct((height, owner_rows), f32)] * 2,
+        in_specs=[pl.BlockSpec(memory_space=pltpu.SMEM), pl.BlockSpec(memory_space=pltpu.VMEM)],
+        out_specs=[pl.BlockSpec(memory_space=pl.ANY)] * 2,
+        scratch_shapes=[
+            stream, stream, pltpu.VMEM((teams, blocks + 2, ROWS, LANES), f32),
+            sky, sky, sky, sky, sky, stream,
+            pltpu.VMEM((teams, NSUB, ROWS, LANES), f32),
+            pltpu.VMEM((wafers, NSUB, ROWS, LANES), f32),
+            pltpu.VMEM((teams, ROWS, LANES), f32),
+            pltpu.VMEM((teams, lag_count, ROWS, LANES), f32),
+            pltpu.VMEM((teams, lag_count, ROWS, LANES), jnp.int32),
+            pltpu.VMEM((total, 2 * LANES), f32),
+            pltpu.VMEM((total, LANES), f32),
+            pltpu.VMEM((2 * LANES, LANES), jnp.int32),
+            pltpu.VMEM((2 * LANES, LANES), f32),
+            pltpu.VMEM((devices, ROWS, LANES), f32),
+            pltpu.VMEM((devices, 2 * ROWS, LANES), jnp.int32),
+            pltpu.VMEM((2 * LANES, LANES), jnp.int32),
+            pltpu.VMEM((total, 2 * height), f32),
+            pltpu.VMEM((slots + ROWS, 2 * height), f32),
+            pltpu.VMEM((slots // LANES + 2, 2 * height, LANES), f32),
+            pltpu.VMEM((2, height, OUT_TILES * LANES), f32),
+            pltpu.VMEM((2, height, OUT_TILES * LANES), f32),
+            pltpu.SMEM((devices, 2 * ROWS, LANES), jnp.int32),
+            pltpu.SMEM((2 * LANES, LANES), jnp.int32),
+            pltpu.SMEM((total,), jnp.int32),
+            pltpu.SemaphoreType.DMA((2,)),
+            pltpu.SemaphoreType.DMA((2,)),
+            pltpu.SemaphoreType.DMA((2,)),
+        ],
+        compiler_params=pltpu.CompilerParams(vmem_limit_bytes=VMEM_BYTES),
+        name="map_maker",
+    )(own, gathered)
+    return x_turned.T, r_turned.T
+
+
+def local(sizes, *arguments):
+    tod, hit_list, band_lag = arguments[0], arguments[3], arguments[7]
+    shape, det_count = part_shape(sizes, tod, hit_list, band_lag)
+    if fits_one_device(shape, det_count):
+        return whole_part(shape, *arguments)
+    return distributed(*arguments)
+
+
 def solution(mesh):
     placed = (
         P(("groups", "wafer"), "det", "rep"),
@@ -163,7 +713,7 @@
         P(("groups", "wafer"), "det", None),
     )
     return jax.shard_map(
-        local,
+        functools.partial(local, mesh.shape),
         mesh=mesh,
         in_specs=placed,
         out_specs=(P(("groups", "det", "wafer"), None), P(("groups", "det", "wafer"), None)),

time: 883 us -> 218 us (0.25)
  other arithmetic: 369 us -> 5.08 us
  blocking collectives: 290 us -> 0 us
  Pallas kernels: 0 us -> 148 us
  local copies, waits for them, and re-layouts: 146 us -> 2.65 us
  starting transfers between devices: 42.4 us -> 0.04 us
  waiting for transfers between devices: 8.71 us -> 44.7 us
    psum x13 -> x0, blocking collectives: 238 us -> none  [the longest x8 136 us: remove_common(): group_sums, group_counts = lax.psum((local_sums, member_count), 'det')]
    pallas_call x0 -> x1, Pallas kernels: none -> 148 us  [whole_part(): pl.pallas_call(functools.partial(whole_part_kernel, shape), out_shape=[ja...]
    reduce_sum x6 -> x1, other arithmetic: 128 us -> 0.8 us  [whole_part(): jnp.sum(jnp.where(found, owner, 0), axis=(0, 1)).reshape(ROWS, tiles)]
    add x11 -> x0, other arithmetic: 103 us -> none  [the longest x2 65.9 us: local(): direction = precond + energy_next / energy * direction]
    unnamed x31 -> x0, local copies, waits for them, and re-layouts: 98.3 us -> none
    scatter-add x5 -> x0, other arithmetic: 84.8 us -> none  [to_owners(): summed = jnp.zeros((owner_rows, block_width), jnp.float32).at[target_rows...]
    all_gather x0 -> x1, waiting for transfers between devices: none -> 44.7 us  [whole_part(): lax.all_gather(payload, ('wafer', 'det', 'rep'), axis=0, tiled=False)]
    all_to_all x3 -> x0, blocking collectives: 37.9 us -> none  [local(): lax.all_to_all(from_blocks, ('det', 'wafer'), split_axis=0, concat_axis=0...]
  transfers between devices with their start and end apart: 14 -> 1, of which waited for: 4 -> 1; matrix products, arithmetic and copies ran while one was open for 9% -> 0% of each run, Pallas kernels for 0% -> 0%
where the time goes in v1:
time: 218 us; the launch traced here: 215 us
  Pallas kernels  148 us (68%)
  waiting for transfers between devices  44.7 us (21%)
  between operations  14.1 us (6%)
  other arithmetic  5.08 us (2%)
  local copies, waits for them, and re-layouts  2.65 us (1%)
    pallas_call x1, Pallas kernels, whole_part(): pl.pallas_call(functools.partial(whole_part_kernel, shape), out_shape=[ja...  148 us
    all_gather x1, waiting for transfers between devices, whole_part(): lax.all_gather(payload, ('wafer', 'det', 'rep'), axis=0, tiled=False)  44.7 us
  transfers between devices with their start and end apart: 1, of which 1 were waited for; matrix products, arithmetic and copies ran while one was open for 0% of the time, Pallas kernels for 0%

profile of v1, /device:TPU:0, one launch (start us, length us, event | category | flops | bytes accessed | tf_op | source)
XLA Modules:
  0.0 214.5 jit_solution(4206334133434268795)
XLA Ops:
  7.2 0.0 all-gather.3.cloned.1.call-start
  7.2 0.7 convert_bitcast_fusion.1
  7.9 0.7 convert_element_type.42
  8.6 0.8 select_reduce_fusion
  9.4 0.8 squeeze.19
  10.1 0.7 convert_bitcast_fusion
  10.8 0.1 copy.17
  10.9 0.1 copy.14
  11.0 0.1 mul.16
  11.1 0.7 fusion.3
  11.8 0.7 copy.15
  12.5 0.8 copy.16
  13.2 0.1 convert_element_type.43
  13.3 0.1 concatenate.9
  13.4 1.5 fusion
  14.9 0.0 all-gather.3.cloned.1.call-update
  15.0 44.7 %all-gather.3.cloned.1.call-done = f32[128,4352]{1,0:T(8,128)} async-done(((f32[8,4352]{1,0:T(8,128)}), f32[128,4352]{1,0:T(8,128)}) %all-gather.3.cloned.1.call-update) | async-done | bytes 2228240 | tf_op jit(solution)/shard_map/all_gather | solution.py:651
  59.6 148.0 %map_maker.1 = (f32[192,24576]{1,0:T(8,128)}, f32[192,24576]{1,0:T(8,128)}) custom-call(s32[1]{0:T(128)} %bitcast.own_ref, f32[16,8,4352]{2,1,0:T(8,128)} %bitcast.21), custom_call_target="tpu_custom_call" | custom-call | tf_op jit(solution)/shard_map/map_maker/pallas_call | solution.py:658
  (2 shorter events, 0.0 us)
Async XLA Ops:
  7.2 52.5 %all-gather.3.cloned.1.call-start = ((), (), s32[]{:S(2)}) async-start(), calls=%async_computation | async-start | bytes 2367488 | tf_op jit(solution)/shard_map/all_gather | solution.py:651
Sparse Core Ops, SparseCore 0:
  15.1 44.5 all-gather.2

commit v2 on v1

--- a/solution.py
+++ b/solution.py
@@ -158,12 +158,23 @@
 LANES = 128
 ROWS = 8
 OUT_TILES = 4
+PAIR_BATCH = 4
 BIG = float(1 << 24)
 VMEM_BYTES = 60 << 20
 
 
 def lane_take(block, index):
     return jnp.take_along_axis(block, index, axis=1, mode="promise_in_bounds")
+
+
+def wide(values):
+    return jnp.broadcast_to(values, (ROWS, LANES))
+
+
+def tile_iotas():
+    lane = lax.broadcasted_iota(jnp.int32, (ROWS, LANES), 1)
+    sub = lax.broadcasted_iota(jnp.int32, (ROWS, LANES), 0)
+    return lane, sub
 
 
 def cosine_sine_double(angle):
@@ -185,98 +196,103 @@
     return first, second
 
 
-def whole_part_kernel(
-    shape, own_ref, part_ref, x_ref, r_ref,
-    cos_ref, sin_ref, clean_ref, inverse_ref, x_map, r_map, d_map, image_map, weight_ref,
-    member_ref, share_ref, base_ref, coef_ref, lag_ref, high_ref, low_ref, place_ref, full_ref,
-    code_ref, table_ref, start_ref, rows_ref, sorted_ref, column_ref, x_buffer, r_buffer,
-    table_smem, start_smem, twin_smem, table_sem, x_sem, r_sem,
+def pack_kernel(shape, row_ref, hit_ref, group_ref, base_ref, coef_ref, lag_ref, out_ref):
+    wafers, dets, reps, tiles, owners, capacity, owner_rows, lag_count = shape
+    lane, sub = tile_iotas()
+    lists = hit_ref[...]
+    owner_hits = jnp.zeros((ROWS, LANES), jnp.float32)
+    for c in range(capacity):
+        owner_hits = owner_hits + jnp.where(wide(lists[:, c : c + 1]) == lane, 1.0, 0.0)
+    owner_of = jnp.sum(owner_hits * sub.astype(jnp.float32), axis=0, keepdims=True)
+    owner_of = lane_take(wide(owner_of), (lane + sub * tiles) & (LANES - 1))
+    spread = jnp.zeros((ROWS, LANES), jnp.float32)
+    rows = row_ref[...].astype(jnp.float32)
+    for b in range(tiles):
+        spread = jnp.where(lane == b, wide(rows[:, b : b + 1]), spread)
+    ids = jnp.where(lane < tiles, owner_of * float(owner_rows) + spread, 0.0)
+
+    def column(row):
+        values = jnp.zeros((ROWS, LANES), jnp.float32)
+        for k in range(ROWS):
+            values = jnp.where(sub == k, wide(row[:, k : k + 1]), values)
+        return values
+
+    table = jnp.where(lane == tiles, column(group_ref[...].astype(jnp.float32)), ids)
+    table = jnp.where(lane == tiles + 1, column(base_ref[...]), table)
+    for j in range(lag_count):
+        at = tiles + 2 + j
+        table = jnp.where(lane == at, column(coef_ref[j : j + 1, :]), table)
+        lag = lag_ref[j : j + 1, :].astype(jnp.float32)
+        table = jnp.where(lane == at + lag_count, column(lag), table)
+    out_ref[:, 0:LANES] = table
+    along = jnp.where((lane & (ROWS - 1)) == sub, lane_take(ids, lane >> 3), 0.0)
+    out_ref[:, LANES : 2 * LANES] = wide(jnp.sum(along, axis=0, keepdims=True))
+    hits = jnp.full((ROWS, LANES), LANES, jnp.int32)
+    for c in range(capacity):
+        number = wide(lists[:, c : c + 1])
+        place = (number & (tiles - 1)) * ROWS + (number >> (tiles.bit_length() - 1))
+        hits = jnp.where(lane == c, jnp.where(number < LANES, place, LANES), hits)
+    out_ref[:, 2 * LANES : 3 * LANES] = hits.astype(jnp.float32)
+
+
+def list_kernel(
+    shape, own_ref, part_ref,
+    weight_ref, place_ref, full_ref, start_ref, size_ref, pair_ref, group_ref, source_ref, target_ref,
+    code_ref, high_ref, low_ref, table_ref, table_smem, table_sem,
 ):
     wafers, dets, reps, tiles, owners, capacity, owner_rows, lag_count = shape
-    teams = wafers * dets
-    devices = teams * reps
+    devices = wafers * dets * reps
     blocks = reps * tiles
     total = devices * tiles * ROWS
-    span = tiles * LANES
-    params = 2 * span
-    extra = params + LANES
-    groups = owner_rows // LANES
-    lane = lax.broadcasted_iota(jnp.int32, (ROWS, LANES), 1)
-    sub = lax.broadcasted_iota(jnp.int32, (ROWS, LANES), 0)
+    slots = devices * capacity
+    lane, sub = tile_iotas()
     lane_f = lane.astype(jnp.float32)
     own = own_ref[0]
     first_row = (own * owner_rows).astype(jnp.float32)
-
-    def wide(column):
-        return jnp.broadcast_to(column, (ROWS, LANES))
-
-    def fold(block):
-        return block + pltpu.roll(block, LANES // 2, 1)
-
-    for team in range(teams):
-        values = part_ref[team * reps, :, params : params + LANES]
-        base_ref[team] = wide(values[:, tiles + 1 : tiles + 2])
-        for group in range(NSUB):
-            member_ref[team, group] = wide(
-                (values[:, tiles : tiles + 1] == float(group)).astype(jnp.float32)
-            )
-        for j in range(lag_count):
-            at = tiles + 2 + j
-            coef_ref[team, j] = wide(values[:, at : at + 1])
-            lag_ref[team, j] = wide(values[:, at + lag_count : at + lag_count + 1].astype(jnp.int32))
-        clean_ref[team, 0] = jnp.zeros((ROWS, LANES), jnp.float32)
-        clean_ref[team, blocks + 1] = jnp.zeros((ROWS, LANES), jnp.float32)
-    for wafer in range(wafers):
-        for group in range(NSUB):
-            count = member_ref[wafer * dets, group]
-            for i in range(1, dets):
-                count = count + member_ref[wafer * dets + i, group]
-            count = jnp.sum(count, axis=0, keepdims=True)
-            share_ref[wafer, group] = wide(1.0 / jnp.maximum(count, 1.0))
-
-    def survey(device, carry):
-        team = device // reps
-        values = part_ref[device, :, params : params + LANES]
-        base = base_ref[team]
+    many = float(total * total)
+
+    def exact_dot(left, right):
+        return jnp.dot(
+            left.astype(jnp.bfloat16), right.astype(jnp.bfloat16),
+            preferred_element_type=jnp.float32,
+        )
+
+    depth = 2 * LANES
+    tall = lax.broadcasted_iota(jnp.int32, (depth, LANES), 0).astype(jnp.float32)
+
+    def survey(device, hits):
+        values = part_ref[device, :, 0:LANES]
         codes = jnp.full((ROWS, LANES), BIG, jnp.float32)
         for b in range(tiles):
             at = device * tiles + b
-            first, second = cosine_sine_double(part_ref[device, :, b * LANES : (b + 1) * LANES])
-            cos_ref[at] = first
-            sin_ref[at] = second
-            image_map[at, 0] = base + base
-            image_map[at, 1] = fold(base * (first * first))
-            image_map[at, 2] = fold(base * (second * second))
             ids = wide(values[:, b : b + 1])
             least = jnp.full((ROWS, LANES), BIG, jnp.float32)
+            matches = jnp.zeros((ROWS, LANES), jnp.float32)
             for other in range(devices):
-                row = part_ref[other, 0:1, extra : extra + LANES]
-                least = jnp.minimum(least, jnp.where(ids == row, lane_f + float(other * LANES), BIG))
+                same = ids == part_ref[other, :, LANES : 2 * LANES]
+                least = jnp.minimum(least, jnp.where(same, lane_f + float(other * LANES), BIG))
+                matches = matches + jnp.where(same, 1.0, 0.0)
             least = jnp.min(least, axis=1, keepdims=True)
-            mine = (device * LANES + sub[:, 0:1] * tiles + b).astype(jnp.float32)
+            matches = jnp.sum(matches, axis=1, keepdims=True)
+            mine = (at * ROWS + sub[:, 0:1]).astype(jnp.float32)
             weight_ref[at] = wide(jnp.where(least == mine, 0.5, 0.0))
-            code = jnp.where(least < mine, mine * float(total) + least, BIG)
+            code = mine * float(total) + least + jnp.where(matches > 2.0, many, 0.0)
+            code = jnp.where(least < mine, code, BIG)
             codes = jnp.where(lane == b, code, codes)
             local_row = ids - first_row
             high = jnp.floor(local_row * (1.0 / LANES))
             low = local_row - high * LANES
             at_row = pl.ds(pl.multiple_of(at * ROWS, ROWS), ROWS)
             high_ref[at_row, 0:LANES] = (high == lane_f).astype(jnp.float32)
-            high_ref[at_row, LANES : 2 * LANES] = (high == lane_f + LANES).astype(jnp.float32)
+            high_ref[at_row, LANES:depth] = (high == lane_f + LANES).astype(jnp.float32)
             low_ref[at_row, :] = (low == lane_f).astype(jnp.float32)
         code_ref[device] = codes
-        return carry
-
-    lax.fori_loop(0, devices, survey, 0)
-
-    def exact_dot(left, right, dims):
-        return lax.dot_general(
-            left.astype(jnp.bfloat16), right.astype(jnp.bfloat16), (dims, ((), ())),
-            preferred_element_type=jnp.float32,
-        )
-
-    depth = 2 * LANES
-    hits = exact_dot(high_ref[...], low_ref[...], ((0,), (0,)))
+        along = jnp.floor((part_ref[device, 0:1, LANES : 2 * LANES] - first_row) * (1.0 / LANES))
+        along = (jnp.broadcast_to(along, (depth, LANES)) == tall).astype(jnp.float32)
+        at_rows = pl.ds(pl.multiple_of(device * LANES, LANES), LANES)
+        return hits + exact_dot(along, low_ref[at_rows, :])
+
+    hits = lax.fori_loop(0, devices, survey, jnp.zeros((depth, LANES), jnp.float32))
     full = jnp.minimum(hits, 1.0)
     full_ref[...] = full
     before = (
@@ -287,10 +303,9 @@
         lax.broadcasted_iota(jnp.int32, (depth, depth), 1)
         < lax.broadcasted_iota(jnp.int32, (depth, depth), 0)
     ).astype(jnp.float32)
-    in_tile = exact_dot(full, before, ((1,), (0,)))
-    tile_sum = exact_dot(full, jnp.ones((LANES, LANES), jnp.float32), ((1,), (0,)))
-    start = exact_dot(above, tile_sum, ((1,), (0,)))
-    place = in_tile + start
+    tile_sum = exact_dot(full, jnp.ones((LANES, LANES), jnp.float32))
+    start = exact_dot(above, tile_sum)
+    place = exact_dot(full, before) + start
     place_ref[...] = place.astype(jnp.int32)
     start_ref[...] = start.astype(jnp.int32)
     place_high = jnp.floor(place * (1.0 / LANES))
@@ -299,28 +314,20 @@
     def rank_of(device, carry):
         at_rows = pl.ds(pl.multiple_of(device * LANES, LANES), LANES)
         high = high_ref[at_rows, :]
-        rank = LANES * exact_dot(high, place_high, ((1,), (0,))) + exact_dot(
-            high, place_low, ((1,), (0,))
-        )
+        rank = LANES * exact_dot(high, place_high) + exact_dot(high, place_low)
         rank = jnp.sum(rank * low_ref[at_rows, :], axis=1, keepdims=True)
         table = jnp.zeros((ROWS, LANES), jnp.float32)
         for b in range(tiles):
             table = jnp.where(lane == b, rank[b * ROWS : (b + 1) * ROWS], table)
         table_ref[device, 0:ROWS] = table.astype(jnp.int32)
-        table_ref[device, ROWS : 2 * ROWS] = part_ref[device, :, extra : extra + LANES].astype(
+        table_ref[device, ROWS : 2 * ROWS] = part_ref[device, :, 2 * LANES : 3 * LANES].astype(
             jnp.int32
         )
         return carry
 
     lax.fori_loop(0, devices, rank_of, 0)
-    copies = (
-        pltpu.make_async_copy(table_ref, table_smem, table_sem.at[0]),
-        pltpu.make_async_copy(start_ref, start_smem, table_sem.at[1]),
-    )
-    for copy in copies:
-        copy.start()
-    for copy in copies:
-        copy.wait()
+    copy = pltpu.make_async_copy(table_ref, table_smem, table_sem.at[0])
+    copy.start()
 
     def next_code(last):
         found = jnp.full((ROWS, LANES), BIG, jnp.float32)
@@ -329,134 +336,252 @@
             found = jnp.minimum(found, jnp.where(codes > last, codes, BIG))
         return jnp.min(found)
 
-    def take_twin(state):
-        count, code = state
-        twin_smem[count] = code.astype(jnp.int32)
-        return count + 1, next_code(code)
-
-    twin_count, _ = lax.while_loop(
-        lambda state: state[1] < BIG, take_twin, (jnp.int32(0), next_code(jnp.float32(-1.0)))
+    def detector(key):
+        return lax.rem(lax.div(key, blocks * ROWS), dets) * ROWS + lax.rem(key, ROWS)
+
+    def take(list_ref, offset):
+        def one(state):
+            count, code = state
+            number = (code - offset).astype(jnp.int32)
+            key = lax.div(number, total)
+            lead = lax.rem(number, total)
+            list_ref[0, count] = key
+            list_ref[1, count] = lead
+            list_ref[2, count] = (3 * (detector(key) - detector(lead))) & (PBLOCK - 1)
+            return count + 1, next_code(code)
+
+        return one
+
+    pairs, code = lax.while_loop(
+        lambda state: state[1] < many, take(pair_ref, 0.0),
+        (jnp.int32(0), next_code(jnp.float32(-1.0))),
     )
-
-    def locate(number):
-        device = lax.div(number, LANES)
-        inside = lax.rem(number, LANES)
-        row = lax.div(inside, tiles)
-        detector = lax.rem(lax.div(device, reps), dets) * ROWS + row
-        return device * tiles + lax.rem(inside, tiles), row, detector
+    grouped, _ = lax.while_loop(
+        lambda state: state[1] < BIG, take(group_ref, many), (jnp.int32(0), code)
+    )
+    batches = lax.div(pairs + PAIR_BATCH - 1, PAIR_BATCH)
+
+    def fill(n, carry):
+        pair_ref[0, n] = total
+        pair_ref[1, n] = total + 1
+        pair_ref[2, n] = 0
+        return carry
+
+    lax.fori_loop(pairs, batches * PAIR_BATCH, fill, 0)
+    size_ref[0] = batches
+    size_ref[1] = grouped
+    copy.wait()
+
+    def pick(device, carry):
+        for c in range(capacity):
+            number = table_smem[device, ROWS + own, c]
+            valid = number < LANES
+            number = jnp.where(valid, number, 0)
+            rank = table_smem[device, number & (ROWS - 1), number >> 3]
+            source_ref[device, c] = device * LANES + number
+            target_ref[device, c] = jnp.where(valid, rank, slots)
+        return carry
+
+    lax.fori_loop(0, devices, pick, 0)
+
+
+def map_kernel(
+    shape, size_ref, pair_ref, group_ref, source_ref, target_ref, start_smem,
+    part_ref, psi_ref, tod_ref, weight_ref, place_ref, full_ref, start_ref, x_ref, r_ref,
+    cos_ref, sin_ref, clean_ref, noise_ref, inverse_ref, x_map, r_map, d_map, image_map,
+    member_ref, share_ref, base_ref, coef_ref, lag_ref,
+    rows_ref, sorted_ref, column_ref, x_buffer, r_buffer, x_sem, r_sem,
+):
+    wafers, dets, reps, tiles, owners, capacity, owner_rows, lag_count = shape
+    teams = wafers * dets
+    devices = teams * reps
+    blocks = reps * tiles
+    count = devices * tiles
+    groups = owner_rows // LANES
+    slots = devices * capacity
+    lane, sub = tile_iotas()
+    zero = jnp.zeros((ROWS, LANES), jnp.float32)
+
+    def fold(block):
+        return block + pltpu.roll(block, LANES // 2, 1)
+
+    def whole_sum(values):
+        values = jnp.sum(values, axis=0, keepdims=True)
+        return wide(jnp.sum(values, axis=1, keepdims=True))
+
+    def loop(times, body, carry, unroll):
+        def several(n, carry):
+            for k in range(unroll):
+                carry = body(n * unroll + k, carry)
+            return carry
+
+        return lax.fori_loop(0, times // unroll, several, carry)
+
+    for team in range(teams):
+        values = part_ref[team * reps, :, 0:LANES]
+        base_ref[team] = wide(values[:, tiles + 1 : tiles + 2])
+        for group in range(NSUB):
+            member_ref[team, group] = wide(
+                (values[:, tiles : tiles + 1] == float(group)).astype(jnp.float32)
+            )
+        for j in range(lag_count):
+            at = tiles + 2 + j
+            coef_ref[team, j] = wide(values[:, at : at + 1])
+            lag_ref[team, j] = wide(values[:, at + lag_count : at + lag_count + 1].astype(jnp.int32))
+        clean_ref[team, 0] = zero
+        clean_ref[team, blocks + 1] = zero
+    for wafer in range(wafers):
+        for group in range(NSUB):
+            members = member_ref[wafer * dets, group]
+            for i in range(1, dets):
+                members = members + member_ref[wafer * dets + i, group]
+            members = jnp.sum(members, axis=0, keepdims=True)
+            share_ref[wafer, group] = wide(1.0 / jnp.maximum(members, 1.0))
+    for c in range(3):
+        image_map[count, c] = zero
+        r_map[count, c] = zero
+
+    def survey(at, carry):
+        device = lax.div(at, tiles)
+        place = pl.ds(pl.multiple_of(lax.rem(at, tiles) * LANES, LANES), LANES)
+        first, second = cosine_sine_double(psi_ref[device, :, place])
+        base = base_ref[lax.div(device, reps)]
+        cos_ref[at] = first
+        sin_ref[at] = second
+        image_map[at, 0] = base + base
+        image_map[at, 1] = fold(base * (first * first))
+        image_map[at, 2] = fold(base * (second * second))
+        return carry
+
+    loop(count, survey, 0, 4)
 
     def merge_twins(target):
+        def pair_batch(n, carry):
+            found = []
+            for k in range(PAIR_BATCH):
+                key, lead, shift = (pair_ref[j, n * PAIR_BATCH + k] for j in range(3))
+                spots = [
+                    (lax.shift_right_logical(spot, 3), pl.ds(spot & (ROWS - 1), 1))
+                    for spot in (key, lead)
+                ]
+                values = [[target[at, c, row, :] for c in range(3)] for at, row in spots]
+                found.append((spots, shift, values))
+            for spots, shift, values in found:
+                turns = (shift, (LANES - shift) & (LANES - 1))
+                for (at, row), own, other, turn in zip(
+                    spots, values, values[::-1], turns[::-1]
+                ):
+                    for c in range(3):
+                        target[at, c, row, :] = own[c] + pltpu.roll(wide(other[c]), turn, 1)[0:1]
+            return carry
+
         def gather_one(n, carry):
-            code = twin_smem[n]
-            at, row, detector = locate(lax.div(code, total))
-            lead_at, lead_row, lead_detector = locate(lax.rem(code, total))
-            shift = (3 * (detector - lead_detector)) & (PBLOCK - 1)
+            key, lead, shift = (group_ref[j, n] for j in range(3))
+            at, row = lax.shift_right_logical(key, 3), key & (ROWS - 1)
+            lead_at, lead_row = lax.shift_right_logical(lead, 3), lead & (ROWS - 1)
             for c in range(3):
                 moved = pltpu.roll(wide(target[at, c, pl.ds(row, 1), :]), shift, 1)
                 target[lead_at, c, pl.ds(lead_row, 1), :] += moved[0:1]
             return carry
 
         def spread_one(n, carry):
-            code = twin_smem[n]
-            at, row, detector = locate(lax.div(code, total))
-            lead_at, lead_row, lead_detector = locate(lax.rem(code, total))
-            shift = (3 * (lead_detector - detector)) & (PBLOCK - 1)
+            key, lead, shift = (group_ref[j, n] for j in range(3))
+            at, row = lax.shift_right_logical(key, 3), key & (ROWS - 1)
+            lead_at, lead_row = lax.shift_right_logical(lead, 3), lead & (ROWS - 1)
+            turn = (LANES - shift) & (LANES - 1)
             for c in range(3):
-                moved = pltpu.roll(wide(target[lead_at, c, pl.ds(lead_row, 1), :]), shift, 1)
+                moved = pltpu.roll(wide(target[lead_at, c, pl.ds(lead_row, 1), :]), turn, 1)
                 target[at, c, pl.ds(row, 1), :] = moved[0:1]
             return carry
 
-        lax.fori_loop(0, twin_count, gather_one, 0)
-        lax.fori_loop(0, twin_count, spread_one, 0)
-
-    def remove_common(wafer, streams):
+        lax.fori_loop(0, size_ref[0], pair_batch, 0)
+        lax.fori_loop(0, size_ref[1], gather_one, 0)
+        lax.fori_loop(0, size_ref[1], spread_one, 0)
+
+    def remove_common(members, shares, streams):
         means = []
         for group in range(NSUB):
-            part = member_ref[wafer * dets, group] * streams[0]
+            part = members[0][group] * streams[0]
             for i in range(1, dets):
-                part = part + member_ref[wafer * dets + i, group] * streams[i]
-            means.append(jnp.sum(part, axis=0, keepdims=True) * share_ref[wafer, group])
+                part = part + members[i][group] * streams[i]
+            means.append(jnp.sum(part, axis=0, keepdims=True) * shares[group])
         result = []
         for i in range(dets):
-            stream = streams[i]
-            for group in range(NSUB):
-                stream = stream - member_ref[wafer * dets + i, group] * means[group]
-            result.append(stream)
+            common = members[i][0] * means[0]
+            for group in range(1, NSUB):
+                common = common + members[i][group] * means[group]
+            result.append(streams[i] - common)
         return result
 
-    def loop(count, body, carry, unroll):
-        def several(n, carry):
-            for k in range(unroll):
-                carry = body(n * unroll + k, carry)
-            return carry
-
-        return lax.fori_loop(0, count // unroll, several, carry)
-
-    def first_removal(stream_of, carry):
+    def removal_pass(stream_of, place, carry):
         for wafer in range(wafers):
+            first = wafer * dets
+            members = [[member_ref[first + i, g] for g in range(NSUB)] for i in range(dets)]
+            shares = [share_ref[wafer, g] for g in range(NSUB)]
 
             def one_time(block, carry):
                 streams = []
                 for i in range(dets):
-                    stream, carry = stream_of(wafer * dets + i, block, carry)
+                    stream, carry = stream_of(first + i, block, carry)
                     streams.append(stream)
-                for i, stream in enumerate(remove_common(wafer, streams)):
-                    clean_ref[wafer * dets + i, block + 1] = stream
+                for i, stream in enumerate(remove_common(members, shares, streams)):
+                    place(first + i, block, stream)
                 return carry
 
             carry = loop(blocks, one_time, carry, 2)
         return carry
 
-    def filter_and_return(target):
-        carry = jnp.zeros((ROWS, LANES), jnp.float32)
-        for wafer in range(wafers):
-
-            def one_time(block, carry):
-                streams = []
-                for i in range(dets):
-                    team = wafer * dets + i
-                    here = clean_ref[team, block + 1]
-                    after = clean_ref[team, block + 2]
-                    ahead = clean_ref[team, block]
-                    result = base_ref[team] * here
-                    for j in range(lag_count):
-                        lag = lag_ref[team, j]
-                        later = lane_take(
-                            jnp.where(lane < lag, after, here), (lane + lag) & (LANES - 1)
-                        )
-                        earlier = lane_take(
-                            jnp.where(lane >= LANES - lag, ahead, here), (lane - lag) & (LANES - 1)
-                        )
-                        result = result + coef_ref[team, j] * (later + earlier)
-                    carry = carry + here * result
-                    streams.append(result)
-                for i, stream in enumerate(remove_common(wafer, streams)):
-                    at = (wafer * dets + i) * blocks + block
-                    target[at, 0] = fold(stream)
-                    target[at, 1] = fold(cos_ref[at] * stream)
-                    target[at, 2] = fold(sin_ref[at] * stream)
-                return carry
-
-            carry = loop(blocks, one_time, carry, 2)
-        return carry
-
-    def whole_sum(values):
-        values = jnp.sum(values, axis=0, keepdims=True)
-        return wide(jnp.sum(values, axis=1, keepdims=True))
-
-    zero = jnp.zeros((ROWS, LANES), jnp.float32)
-    count = teams * blocks
+    def keep_clean(team, block, stream):
+        clean_ref[team, block + 1] = stream
+
+    def filter_pass():
+        def one_team(team, carry):
+            base = base_ref[team]
+            coefs = [coef_ref[team, j] for j in range(lag_count)]
+            lags = [lag_ref[team, j] for j in range(lag_count)]
+            later_turns = [(lane + lag) & (LANES - 1) for lag in lags]
+            earlier_turns = [(lane - lag) & (LANES - 1) for lag in lags]
+
+            def one_time(block, state):
+                ahead, here, carry = state
+                after = clean_ref[team, block + 2]
+                result = base * here
+                for j in range(lag_count):
+                    later = lane_take(jnp.where(lane < lags[j], after, here), later_turns[j])
+                    earlier = lane_take(
+                        jnp.where(lane >= LANES - lags[j], ahead, here), earlier_turns[j]
+                    )
+                    result = result + coefs[j] * (later + earlier)
+                noise_ref[team * blocks + block] = result
+                return here, after, carry + here * result
+
+            return loop(blocks, one_time, (clean_ref[team, 0], clean_ref[team, 1], carry), 4)[2]
+
+        return lax.fori_loop(0, teams, one_team, zero)
+
+    def return_pass(target):
+        def noise_stream(team, block, carry):
+            return noise_ref[team * blocks + block], carry
+
+        def add_back(team, block, stream):
+            at = team * blocks + block
+            target[at, 0] = fold(stream)
+            target[at, 1] = fold(cos_ref[at] * stream)
+            target[at, 2] = fold(sin_ref[at] * stream)
+
+        removal_pass(noise_stream, add_back, 0)
+        merge_twins(target)
 
     merge_twins(image_map)
 
     def data_stream(team, block, carry):
         device = team * reps + lax.div(block, tiles)
-        at = pl.multiple_of(span + lax.rem(block, tiles) * LANES, LANES)
-        return part_ref[device, :, pl.ds(at, LANES)], carry
-
-    first_removal(data_stream, 0)
-    filter_and_return(r_map)
-    merge_twins(r_map)
+        at = pl.multiple_of(lax.rem(block, tiles) * LANES, LANES)
+        return tod_ref[device, :, pl.ds(at, LANES)], carry
+
+    removal_pass(data_stream, keep_clean, 0)
+    filter_pass()
+    return_pass(r_map)
 
     def begin(at, carry):
         parts = zero
@@ -467,7 +592,7 @@
             parts = parts + residual * (inverse * residual)
         return carry + weight_ref[at] * parts
 
-    energy = whole_sum(loop(count, begin, zero, 2))
+    energy = whole_sum(loop(count, begin, zero, 4))
     factor = zero
     for iteration in range(ITERS):
         last = iteration == ITERS - 1
@@ -485,9 +610,9 @@
             stream = parts[0] + cos_ref[at] * parts[1] + sin_ref[at] * parts[2]
             return stream, carry + weight_ref[at] * squares
 
-        prior = first_removal(seen_stream, zero)
-        product = filter_and_return(image_map)
-        merge_twins(image_map)
+        prior = removal_pass(seen_stream, keep_clean, zero)
+        product = filter_pass()
+        return_pass(image_map)
         step = energy / whole_sum(product + prior_weight * prior)
 
         def advance(at):
@@ -511,7 +636,7 @@
                     parts = parts + new_r[c] * (inverse_ref[at, c] * new_r[c])
                 return carry + weight_ref[at] * parts
 
-            next_energy = whole_sum(loop(count, update, zero, 2))
+            next_energy = whole_sum(loop(count, update, zero, 4))
             factor = next_energy / energy
             energy = next_energy
         else:
@@ -528,22 +653,11 @@
                     )
                 return carry
 
-            loop(count, place_pixels, 0, 2)
-
-    slots = devices * capacity
-    flat = own * capacity
-    hit_row = ROWS + 1 + lax.div(flat, LANES)
-    hit_lane = lax.rem(flat, LANES)
+            loop(count, place_pixels, 0, 4)
 
     def pick(device, carry):
         for c in range(capacity):
-            number = table_smem[device, hit_row, hit_lane + c]
-            valid = number < LANES
-            number = jnp.where(valid, number, 0)
-            row = lax.div(number, tiles)
-            column = lax.rem(number, tiles)
-            source = (device * tiles + column) * ROWS + row
-            target = jnp.where(valid, table_smem[device, row, column], slots)
+            source, target = source_ref[device, c], target_ref[device, c]
             sorted_ref[pl.ds(target, 1), :] = rows_ref[pl.ds(source, 1), :]
         return carry
 
@@ -607,20 +721,18 @@
     wafers, dets, reps, tiles, owners, capacity, owner_rows, lag_count = shape
     devices = wafers * dets * reps
     total = devices * tiles * det_count
-    table_rows = owners * capacity // LANES
     groups = owner_rows // LANES
     return (
         det_count == ROWS
+        and owners == ROWS
         and tiles * ROWS == LANES
         and tiles + 2 + 2 * lag_count <= LANES
-        and reps * tiles % 2 == 0
-        and owners * capacity % LANES == 0
-        and LANES % capacity == 0
-        and table_rows < ROWS
+        and reps * tiles % 4 == 0
+        and capacity <= LANES
         and devices * capacity % LANES == 0
         and owner_rows % (LANES * OUT_TILES) == 0
         and 2 * OUT_TILES <= groups <= 2 * LANES
-        and total * total < BIG
+        and 2 * total * total <= BIG
     )
 
 
@@ -632,64 +744,80 @@
     count = devices * tiles
     total = count * ROWS
     slots = devices * capacity
-    table = hit_list[0, 0, 0]
-    found = table[:, :, None] == jnp.arange(LANES, dtype=jnp.int32)[None, None, :]
-    owner = jnp.arange(owners, dtype=jnp.int32)[:, None, None]
-    owner_of = jnp.sum(jnp.where(found, owner, 0), axis=(0, 1)).reshape(ROWS, tiles)
-    ids = (owner_of * owner_rows + point_row[0]).astype(jnp.float32)
-    per_detector = jnp.concatenate(
-        [
-            ids, group_id[0][:, None].astype(jnp.float32), a_zero[0][:, None], band_coef[0],
-            band_lag[0].astype(jnp.float32),
+    height = 3 * PBLOCK
+    f32, i32 = jnp.float32, jnp.int32
+    part_axes = ("wafer", "det", "rep")
+    vmem, smem = pl.BlockSpec(memory_space=pltpu.VMEM), pl.BlockSpec(memory_space=pltpu.SMEM)
+    params = pltpu.CompilerParams(vmem_limit_bytes=VMEM_BYTES)
+    tables = pl.pallas_call(
+        functools.partial(pack_kernel, shape),
+        out_shape=jax.ShapeDtypeStruct((ROWS, 3 * LANES), f32),
+        in_specs=[vmem] * 6,
+        out_specs=vmem,
+        compiler_params=params,
+        name="pack",
+    )(point_row[0], hit_list[0, 0, 0], group_id, a_zero, band_coef[0].T, band_lag[0].T)
+    tables = lax.all_gather(tables, part_axes, axis=0, tiled=False)
+    angles = lax.all_gather(psi, part_axes, axis=0, tiled=True)
+    samples = lax.all_gather(tod, part_axes, axis=0, tiled=True)
+    own = (lax.axis_index("det") * wafers + lax.axis_index("wafer")).astype(i32).reshape(1)
+    weight, place, full, start, size, pair, group, source, target = pl.pallas_call(
+        functools.partial(list_kernel, shape),
+        out_shape=[
+            jax.ShapeDtypeStruct((count, ROWS, LANES), f32),
+            jax.ShapeDtypeStruct((2 * LANES, LANES), i32),
+            jax.ShapeDtypeStruct((2 * LANES, LANES), f32),
+            jax.ShapeDtypeStruct((2 * LANES, LANES), i32),
+            jax.ShapeDtypeStruct((2,), i32),
+            jax.ShapeDtypeStruct((3, total), i32),
+            jax.ShapeDtypeStruct((3, total), i32),
+            jax.ShapeDtypeStruct((devices, capacity), i32),
+            jax.ShapeDtypeStruct((devices, capacity), i32),
         ],
-        axis=1,
-    )
-    per_detector = jnp.pad(per_detector, ((0, 0), (0, LANES - per_detector.shape[1])))
-    tables = jnp.concatenate([ids.reshape(-1), table.reshape(-1).astype(jnp.float32)])
-    tables = jnp.pad(tables, (0, ROWS * LANES - tables.shape[0])).reshape(ROWS, LANES)
-    payload = jnp.concatenate([psi[0], tod[0], per_detector, tables], axis=1)
-    gathered = lax.all_gather(payload, ("wafer", "det", "rep"), axis=0, tiled=False)
-    own = (lax.axis_index("det") * wafers + lax.axis_index("wafer")).astype(jnp.int32).reshape(1)
-
-    height = 3 * PBLOCK
-    f32 = jnp.float32
+        in_specs=[smem, vmem],
+        out_specs=[vmem] * 4 + [smem] * 5,
+        scratch_shapes=[
+            pltpu.VMEM((devices, ROWS, LANES), f32),
+            pltpu.VMEM((total, 2 * LANES), f32),
+            pltpu.VMEM((total, LANES), f32),
+            pltpu.VMEM((devices, 2 * ROWS, LANES), i32),
+            pltpu.SMEM((devices, 2 * ROWS, LANES), i32),
+            pltpu.SemaphoreType.DMA((1,)),
+        ],
+        compiler_params=params,
+        cost_estimate=pl.CostEstimate(flops=10**9, bytes_accessed=4 * 10**6, transcendentals=0),
+        name="lists",
+    )(own, tables)
     stream = pltpu.VMEM((count, ROWS, LANES), f32)
     sky = pltpu.VMEM((count, 3, ROWS, LANES), f32)
+    sky_and_spare = pltpu.VMEM((count + 1, 3, ROWS, LANES), f32)
     x_turned, r_turned = pl.pallas_call(
-        functools.partial(whole_part_kernel, shape),
+        functools.partial(map_kernel, shape),
         out_shape=[jax.ShapeDtypeStruct((height, owner_rows), f32)] * 2,
-        in_specs=[pl.BlockSpec(memory_space=pltpu.SMEM), pl.BlockSpec(memory_space=pltpu.VMEM)],
+        in_specs=[smem] * 6 + [vmem] * 7,
         out_specs=[pl.BlockSpec(memory_space=pl.ANY)] * 2,
         scratch_shapes=[
-            stream, stream, pltpu.VMEM((teams, blocks + 2, ROWS, LANES), f32),
-            sky, sky, sky, sky, sky, stream,
+            stream, stream, pltpu.VMEM((teams, blocks + 2, ROWS, LANES), f32), stream,
+            sky, sky, sky_and_spare, sky, sky_and_spare,
             pltpu.VMEM((teams, NSUB, ROWS, LANES), f32),
             pltpu.VMEM((wafers, NSUB, ROWS, LANES), f32),
             pltpu.VMEM((teams, ROWS, LANES), f32),
             pltpu.VMEM((teams, lag_count, ROWS, LANES), f32),
-            pltpu.VMEM((teams, lag_count, ROWS, LANES), jnp.int32),
-            pltpu.VMEM((total, 2 * LANES), f32),
-            pltpu.VMEM((total, LANES), f32),
-            pltpu.VMEM((2 * LANES, LANES), jnp.int32),
-            pltpu.VMEM((2 * LANES, LANES), f32),
-            pltpu.VMEM((devices, ROWS, LANES), f32),
-            pltpu.VMEM((devices, 2 * ROWS, LANES), jnp.int32),
-            pltpu.VMEM((2 * LANES, LANES), jnp.int32),
+            pltpu.VMEM((teams, lag_count, ROWS, LANES), i32),
             pltpu.VMEM((total, 2 * height), f32),
             pltpu.VMEM((slots + ROWS, 2 * height), f32),
             pltpu.VMEM((slots // LANES + 2, 2 * height, LANES), f32),
             pltpu.VMEM((2, height, OUT_TILES * LANES), f32),
             pltpu.VMEM((2, height, OUT_TILES * LANES), f32),
-            pltpu.SMEM((devices, 2 * ROWS, LANES), jnp.int32),
-            pltpu.SMEM((2 * LANES, LANES), jnp.int32),
-            pltpu.SMEM((total,), jnp.int32),
-            pltpu.SemaphoreType.DMA((2,)),
             pltpu.SemaphoreType.DMA((2,)),
             pltpu.SemaphoreType.DMA((2,)),
         ],
-        compiler_params=pltpu.CompilerParams(vmem_limit_bytes=VMEM_BYTES),
+        compiler_params=params,
         name="map_maker",
-    )(own, gathered)
+    )(
+        size, pair, group, source, target, start[:, 0:1], tables, angles, samples, weight, place,
+        full, start,
+    )
     return x_turned.T, r_turned.T
 
 

time: 218 us -> 215 us (0.986); the launches traced: 215 us -> 215 us
  blocking collectives: 0 us -> 25.6 us
  waiting for transfers between devices: 44.7 us -> 34 us
  Pallas kernels: 148 us -> 141 us
  other arithmetic: 5.08 us -> 0 us
  local copies, waits for them, and re-layouts: 2.65 us -> 0 us
    all_gather x0 -> x1, blocking collectives: none -> 25.6 us  [whole_part(): tables = lax.all_gather(tables, part_axes, axis=0, tiled=False)]
    all_gather x1 -> x2, waiting for transfers between devices: 44.7 us -> 32.6 us  [the longest x1 32.6 us: whole_part(): angles = lax.all_gather(psi, part_axes, axis=0, tiled=True)]
    pallas_call x1 -> x3, Pallas kernels: 148 us -> 141 us  [the longest x1 118 us: whole_part(): pl.pallas_call(functools.partial(map_kernel, shape), out_shape=[jax.Shape...]
    convert_element_type x5 -> x0, other arithmetic: 2.73 us -> none  [the longest x2 0.7 us: whole_part(): ids = (owner_of * owner_rows + point_row[0]).astype(jnp.float32)]
  transfers between devices with their start and end apart: 1 -> 2, of which waited for: 1 -> 1; matrix products, arithmetic and copies ran while one was open for 0% -> 0% of each run, Pallas kernels for 0% -> 11%
where the time goes in v2:
time: 215 us
  Pallas kernels  141 us (66%)
  waiting for transfers between devices  34 us (16%)
  blocking collectives  25.6 us (12%)
  between operations  14.1 us (7%)
    pallas_call x1, Pallas kernels, whole_part(): pl.pallas_call(functools.partial(map_kernel, shape), out_shape=[jax.Shape...  118 us
    all_gather x1, waiting for transfers between devices, whole_part(): angles = lax.all_gather(psi, part_axes, axis=0, tiled=True)  32.6 us
    all_gather x1, blocking collectives, whole_part(): tables = lax.all_gather(tables, part_axes, axis=0, tiled=False)  25.6 us
    pallas_call x1, Pallas kernels, whole_part(): pl.pallas_call(functools.partial(list_kernel, shape), out_shape=[jax.Shap...  21.7 us
  transfers between devices with their start and end apart: 2, of which 1 were waited for; matrix products, arithmetic and copies ran while one was open for 0% of the time, Pallas kernels for 11%

profile of v2, /device:TPU:0, one launch (start us, length us, event | category | flops | bytes accessed | tf_op | source)
XLA Modules:
  0.0 214.9 jit_solution(663977982047553380)
XLA Ops:
  7.2 0.0 all-gather.6.cloned.1.call-start
  7.2 0.7 all-gather.6.cloned.1.call-update
  7.9 0.0 all-gather.4.cloned.1.call-start
  7.9 0.7 all-gather.4.cloned.1.call-update
  8.7 1.7 pack.1
  10.3 25.6 %all-gather = f32[128,384]{1,0:T(8,128)} all-gather(f32[8,384]{1,0:T(8,128)} %pack.1), channel_id=2, replica_groups=mesh['groups'=2,'det'=4,'wafer'=2,'rep'=2] {'wafer','det','rep'}, dimensions={0}, use_global_device_ids=true | all-gather | bytes 208896 | tf_op jit(solution)/shard_map/all_gather | solution.py:760
  35.9 21.7 %lists.1 = (f32[256,8,128]{2,1,0:T(8,128)}, s32[256,128]{1,0:T(8,128)}, f32[256,128]{1,0:T(8,128)}, s32[256,128]{1,0:T(8,128)}, s32[2]{0:T(128)}, /*index=5*/s32...) custom-call(s32[1]{0:T(128)} %bitcast.own_ref, f32[16,8,384]{2,1,0:T(8,128)} %bitcast.13), custom_call_target="tpu_custom_call" | custom-call | flops 1000000000 | bytes 4000000 | tf_op jit(solution)/shard_map/lists/pallas_call | solution.py:764
  57.5 0.0 all-gather.6.cloned.1.call-done.tod_ref
  57.6 32.6 %all-gather.4.cloned.1.call-done.psi_ref = f32[16,8,2048]{2,1,0:T(8,128)} async-done(((f32[1,8,2048]{2,1,0:T(8,128)}), f32[16,8,2048]{2,1,0:T(8,128)}) %all-gather.4.cloned.1.call-update) | async-done | bytes 1048592 | tf_op jit(solution)/shard_map/all_gather | solution.py:761
  90.1 117.9 %map_maker.1 = (f32[192,24576]{1,0:T(8,128)}, f32[192,24576]{1,0:T(8,128)}) custom-call(s32[2]{0:T(128)} %get-tuple-element.13.size_ref, s32[3,2048]{1,0:T(4,128)} %get-tuple-element.14.pair_ref, s32[3,2048]{1,0:T(4,128)} %get-tuple-element.15.group_ref, s32[16,32]{1,0:T(8,128)} %get-tuple-element.16.source_ref, s32[16,32]{1,0:T(8,128)} %get-tuple-element.17.target_ref, ...), custom_call_target="tpu_custom_call" | custom-call | tf_op jit(solution)/shard_map/map_maker/pallas_call | solution.py:794
Async XLA Ops:
  7.2 50.4 %all-gather.6.cloned.1.call-start = ((), (), s32[]{:S(2)}) async-start(), calls=%async_computation.1 | async-start | bytes 1114112 | tf_op jit(solution)/shard_map/all_gather | solution.py:762
  7.9 82.2 %all-gather.4.cloned.1.call-start = ((), (), s32[]{:S(2)}) async-start(), calls=%async_computation | async-start | bytes 1114112 | tf_op jit(solution)/shard_map/all_gather | solution.py:761
Sparse Core Ops, SparseCore 0:
  10.2 40.7 all-gather.5
  53.2 36.8 all-gather.3

commit v3 on v2

--- a/solution.py
+++ b/solution.py
@@ -159,6 +159,7 @@
 ROWS = 8
 OUT_TILES = 4
 PAIR_BATCH = 4
+TIME_BATCH = 4
 BIG = float(1 << 24)
 VMEM_BYTES = 60 << 20
 
@@ -196,9 +197,13 @@
     return first, second
 
 
-def pack_kernel(shape, row_ref, hit_ref, group_ref, base_ref, coef_ref, lag_ref, out_ref):
+def pack_kernel(
+    shape, angle_ref, row_ref, hit_ref, group_ref, base_ref, coef_ref, lag_ref, out_ref
+):
     wafers, dets, reps, tiles, owners, capacity, owner_rows, lag_count = shape
     lane, sub = tile_iotas()
+    span = tiles * LANES
+    out_ref[:, 0:span] = angle_ref[...]
     lists = hit_ref[...]
     owner_hits = jnp.zeros((ROWS, LANES), jnp.float32)
     for c in range(capacity):
@@ -224,32 +229,70 @@
         table = jnp.where(lane == at, column(coef_ref[j : j + 1, :]), table)
         lag = lag_ref[j : j + 1, :].astype(jnp.float32)
         table = jnp.where(lane == at + lag_count, column(lag), table)
-    out_ref[:, 0:LANES] = table
+    out_ref[:, span : span + LANES] = table
     along = jnp.where((lane & (ROWS - 1)) == sub, lane_take(ids, lane >> 3), 0.0)
-    out_ref[:, LANES : 2 * LANES] = wide(jnp.sum(along, axis=0, keepdims=True))
+    out_ref[:, span + LANES : span + 2 * LANES] = wide(jnp.sum(along, axis=0, keepdims=True))
     hits = jnp.full((ROWS, LANES), LANES, jnp.int32)
     for c in range(capacity):
         number = wide(lists[:, c : c + 1])
         place = (number & (tiles - 1)) * ROWS + (number >> (tiles.bit_length() - 1))
         hits = jnp.where(lane == c, jnp.where(number < LANES, place, LANES), hits)
-    out_ref[:, 2 * LANES : 3 * LANES] = hits.astype(jnp.float32)
+    out_ref[:, span + 2 * LANES : span + 3 * LANES] = hits.astype(jnp.float32)
+
+
+def tile_limit(shape):
+    wafers, dets, reps, tiles, owners, capacity = shape[:6]
+    return 2 * (wafers * dets * reps * capacity // LANES) + 1
+
+
+def part_copies(shape, place_ref, own_refs, columns, to_ref, sem):
+    wafers, dets, reps = shape[:3]
+    here_ref, across_ref, other_ref = own_refs
+    copies = []
+    for swap_rep in range(reps):
+        for swap_wafer in range(wafers):
+            for shift in range(dets):
+                if swap_rep:
+                    source = other_ref.at[swap_wafer, shift]
+                else:
+                    source = (across_ref if swap_wafer else here_ref).at[shift]
+                wafer = place_ref[0] ^ swap_wafer
+                det = place_ref[1] - shift
+                det = jnp.where(det < 0, det + dets, det)
+                rep = place_ref[2] ^ swap_rep
+                device = (wafer * dets + det) * reps + rep
+                copies.append(
+                    pltpu.make_async_copy(
+                        source.at[:, columns], to_ref.at[device], sem.at[len(copies)]
+                    )
+                )
+    return copies
 
 
 def list_kernel(
-    shape, own_ref, part_ref,
-    weight_ref, place_ref, full_ref, start_ref, size_ref, pair_ref, group_ref, source_ref, target_ref,
-    code_ref, high_ref, low_ref, table_ref, table_smem, table_sem,
+    shape, self_ref, here_ref, across_ref, other_ref,
+    weight_ref, place_ref, full_ref, size_ref, pair_ref, group_ref, source_ref, target_ref, start_ref,
+    part_ref, code_ref, high_ref, low_ref, table_ref, count_ref, table_smem, count_smem, part_sem,
+    table_sem,
 ):
     wafers, dets, reps, tiles, owners, capacity, owner_rows, lag_count = shape
     devices = wafers * dets * reps
     blocks = reps * tiles
     total = devices * tiles * ROWS
-    slots = devices * capacity
     lane, sub = tile_iotas()
     lane_f = lane.astype(jnp.float32)
-    own = own_ref[0]
+    own = self_ref[1] * wafers + self_ref[0]
     first_row = (own * owner_rows).astype(jnp.float32)
     many = float(total * total)
+    span = tiles * LANES
+    copies = part_copies(
+        shape, self_ref, (here_ref, across_ref, other_ref), pl.ds(span, 3 * LANES), part_ref,
+        part_sem,
+    )
+    for copy in copies:
+        copy.start()
+    for copy in copies:
+        copy.wait()
 
     def exact_dot(left, right):
         return jnp.dot(
@@ -295,31 +338,29 @@
     hits = lax.fori_loop(0, devices, survey, jnp.zeros((depth, LANES), jnp.float32))
     full = jnp.minimum(hits, 1.0)
     full_ref[...] = full
+    counts = lax.dot_general(
+        jnp.ones((ROWS, LANES), jnp.bfloat16), full.astype(jnp.bfloat16), (((1,), (1,)), ((), ())),
+        preferred_element_type=jnp.float32,
+    )
+    count_ref[...] = counts.astype(jnp.int32)
+    count_copy = pltpu.make_async_copy(count_ref, count_smem, table_sem.at[1])
+    count_copy.start()
     before = (
         lax.broadcasted_iota(jnp.int32, (LANES, LANES), 0)
         < lax.broadcasted_iota(jnp.int32, (LANES, LANES), 1)
     ).astype(jnp.float32)
-    above = (
-        lax.broadcasted_iota(jnp.int32, (depth, depth), 1)
-        < lax.broadcasted_iota(jnp.int32, (depth, depth), 0)
-    ).astype(jnp.float32)
-    tile_sum = exact_dot(full, jnp.ones((LANES, LANES), jnp.float32))
-    start = exact_dot(above, tile_sum)
-    place = exact_dot(full, before) + start
+    place = exact_dot(full, before)
     place_ref[...] = place.astype(jnp.int32)
-    start_ref[...] = start.astype(jnp.int32)
-    place_high = jnp.floor(place * (1.0 / LANES))
-    place_low = place - place_high * LANES
 
     def rank_of(device, carry):
         at_rows = pl.ds(pl.multiple_of(device * LANES, LANES), LANES)
-        high = high_ref[at_rows, :]
-        rank = LANES * exact_dot(high, place_high) + exact_dot(high, place_low)
-        rank = jnp.sum(rank * low_ref[at_rows, :], axis=1, keepdims=True)
+        inside = exact_dot(high_ref[at_rows, :], place)
+        inside = jnp.sum(inside * low_ref[at_rows, :], axis=1, keepdims=True)
         table = jnp.zeros((ROWS, LANES), jnp.float32)
         for b in range(tiles):
-            table = jnp.where(lane == b, rank[b * ROWS : (b + 1) * ROWS], table)
-        table_ref[device, 0:ROWS] = table.astype(jnp.int32)
+            table = jnp.where(lane == b, inside[b * ROWS : (b + 1) * ROWS], table)
+        high = jnp.floor((part_ref[device, :, 0:LANES] - first_row) * (1.0 / LANES))
+        table_ref[device, 0:ROWS] = (table + high * LANES).astype(jnp.int32)
         table_ref[device, ROWS : 2 * ROWS] = part_ref[device, :, 2 * LANES : 3 * LANES].astype(
             jnp.int32
         )
@@ -370,6 +411,15 @@
     lax.fori_loop(pairs, batches * PAIR_BATCH, fill, 0)
     size_ref[0] = batches
     size_ref[1] = grouped
+    count_copy.wait()
+
+    def set_start(group, used):
+        number = count_smem[0, group]
+        start = jnp.where((used & (LANES - 1)) + number > LANES, (used + LANES - 1) & -LANES, used)
+        start_ref[group] = start
+        return start + number
+
+    size_ref[2] = lax.fori_loop(0, owner_rows // LANES, set_start, jnp.int32(0))
     copy.wait()
 
     def pick(device, carry):
@@ -378,27 +428,27 @@
             valid = number < LANES
             number = jnp.where(valid, number, 0)
             rank = table_smem[device, number & (ROWS - 1), number >> 3]
+            group = jnp.where(valid, rank >> 7, 0)
+            target = start_ref[group] + (rank & (LANES - 1))
             source_ref[device, c] = device * LANES + number
-            target_ref[device, c] = jnp.where(valid, rank, slots)
+            target_ref[device, c] = jnp.where(valid, target, tile_limit(shape) * LANES)
         return carry
 
     lax.fori_loop(0, devices, pick, 0)
 
 
 def map_kernel(
-    shape, size_ref, pair_ref, group_ref, source_ref, target_ref, start_smem,
-    part_ref, psi_ref, tod_ref, weight_ref, place_ref, full_ref, start_ref, x_ref, r_ref,
-    cos_ref, sin_ref, clean_ref, noise_ref, inverse_ref, x_map, r_map, d_map, image_map,
+    shape, self_ref, size_ref, pair_ref, group_ref, source_ref, target_ref,
+    here_ref, across_ref, other_ref, tod_here_ref, tod_across_ref, tod_other_ref, weight_ref,
+    column_ref, part_ref, tod_ref, cos_ref, sin_ref, clean_ref, noise_ref, inverse_ref, x_map, r_map, d_map, image_map,
     member_ref, share_ref, base_ref, coef_ref, lag_ref,
-    rows_ref, sorted_ref, column_ref, x_buffer, r_buffer, x_sem, r_sem,
+    rows_ref, sorted_ref, part_sem, tod_sem,
 ):
     wafers, dets, reps, tiles, owners, capacity, owner_rows, lag_count = shape
     teams = wafers * dets
     devices = teams * reps
     blocks = reps * tiles
     count = devices * tiles
-    groups = owner_rows // LANES
-    slots = devices * capacity
     lane, sub = tile_iotas()
     zero = jnp.zeros((ROWS, LANES), jnp.float32)
 
@@ -417,8 +467,21 @@
 
         return lax.fori_loop(0, times // unroll, several, carry)
 
+    span = tiles * LANES
+    part_moves = part_copies(
+        shape, self_ref, (here_ref, across_ref, other_ref), pl.ds(0, span + LANES), part_ref, part_sem
+    )
+    tod_moves = part_copies(
+        shape, self_ref, (tod_here_ref, tod_across_ref, tod_other_ref), pl.ds(0, span), tod_ref,
+        tod_sem,
+    )
+    for copy in part_moves + tod_moves:
+        copy.start()
+    for copy in part_moves:
+        copy.wait()
+
     for team in range(teams):
-        values = part_ref[team * reps, :, 0:LANES]
+        values = part_ref[team * reps, :, span : span + LANES]
         base_ref[team] = wide(values[:, tiles + 1 : tiles + 2])
         for group in range(NSUB):
             member_ref[team, group] = wide(
@@ -444,7 +507,7 @@
     def survey(at, carry):
         device = lax.div(at, tiles)
         place = pl.ds(pl.multiple_of(lax.rem(at, tiles) * LANES, LANES), LANES)
-        first, second = cosine_sine_double(psi_ref[device, :, place])
+        first, second = cosine_sine_double(part_ref[device, :, place])
         base = base_ref[lax.div(device, reps)]
         cos_ref[at] = first
         sin_ref[at] = second
@@ -453,7 +516,7 @@
         image_map[at, 2] = fold(base * (second * second))
         return carry
 
-    loop(count, survey, 0, 4)
+    loop(count, survey, 0, 8)
 
     def merge_twins(target):
         def pair_batch(n, carry):
@@ -498,37 +561,41 @@
         lax.fori_loop(0, size_ref[1], gather_one, 0)
         lax.fori_loop(0, size_ref[1], spread_one, 0)
 
-    def remove_common(members, shares, streams):
-        means = []
-        for group in range(NSUB):
-            part = members[0][group] * streams[0]
-            for i in range(1, dets):
-                part = part + members[i][group] * streams[i]
-            means.append(jnp.sum(part, axis=0, keepdims=True) * shares[group])
-        result = []
-        for i in range(dets):
-            common = members[i][0] * means[0]
-            for group in range(1, NSUB):
-                common = common + members[i][group] * means[group]
-            result.append(streams[i] - common)
-        return result
+    def over_detectors(values):
+        for turn in (4, 2, 1):
+            values = values + pltpu.roll(values, turn, 0)
+        return values
 
     def removal_pass(stream_of, place, carry):
         for wafer in range(wafers):
             first = wafer * dets
-            members = [[member_ref[first + i, g] for g in range(NSUB)] for i in range(dets)]
-            shares = [share_ref[wafer, g] for g in range(NSUB)]
-
-            def one_time(block, carry):
-                streams = []
+
+            def some_times(batch, carry):
+                times = [batch * TIME_BATCH + k for k in range(TIME_BATCH)]
+                streams, parts = [], [[None] * NSUB for _ in times]
                 for i in range(dets):
-                    stream, carry = stream_of(first + i, block, carry)
-                    streams.append(stream)
-                for i, stream in enumerate(remove_common(members, shares, streams)):
-                    place(first + i, block, stream)
+                    members = [member_ref[first + i, g] for g in range(NSUB)]
+                    streams.append([])
+                    for k, block in enumerate(times):
+                        stream, carry = stream_of(first + i, block, carry)
+                        streams[i].append(stream)
+                        for g in range(NSUB):
+                            term = members[g] * stream
+                            parts[k][g] = term if i == 0 else parts[k][g] + term
+                means = [
+                    [over_detectors(parts[k][g]) * share_ref[wafer, g] for g in range(NSUB)]
+                    for k in range(TIME_BATCH)
+                ]
+                for i in range(dets):
+                    members = [member_ref[first + i, g] for g in range(NSUB)]
+                    for k, block in enumerate(times):
+                        common = members[0] * means[k][0]
+                        for g in range(1, NSUB):
+                            common = common + members[g] * means[k][g]
+                        place(first + i, block, streams[i][k] - common)
                 return carry
 
-            carry = loop(blocks, one_time, carry, 2)
+            carry = lax.fori_loop(0, blocks // TIME_BATCH, some_times, carry)
         return carry
 
     def keep_clean(team, block, stream):
@@ -555,7 +622,7 @@
                 noise_ref[team * blocks + block] = result
                 return here, after, carry + here * result
 
-            return loop(blocks, one_time, (clean_ref[team, 0], clean_ref[team, 1], carry), 4)[2]
+            return loop(blocks, one_time, (clean_ref[team, 0], clean_ref[team, 1], carry), 8)[2]
 
         return lax.fori_loop(0, teams, one_team, zero)
 
@@ -573,6 +640,9 @@
         merge_twins(target)
 
     merge_twins(image_map)
+
+    for copy in tod_moves:
+        copy.wait()
 
     def data_stream(team, block, carry):
         device = team * reps + lax.div(block, tiles)
@@ -592,7 +662,7 @@
             parts = parts + residual * (inverse * residual)
         return carry + weight_ref[at] * parts
 
-    energy = whole_sum(loop(count, begin, zero, 4))
+    energy = whole_sum(loop(count, begin, zero, 8))
     factor = zero
     for iteration in range(ITERS):
         last = iteration == ITERS - 1
@@ -636,7 +706,7 @@
                     parts = parts + new_r[c] * (inverse_ref[at, c] * new_r[c])
                 return carry + weight_ref[at] * parts
 
-            next_energy = whole_sum(loop(count, update, zero, 4))
+            next_energy = whole_sum(loop(count, update, zero, 8))
             factor = next_energy / energy
             energy = next_energy
         else:
@@ -653,7 +723,7 @@
                     )
                 return carry
 
-            loop(count, place_pixels, 0, 4)
+            loop(count, place_pixels, 0, 8)
 
     def pick(device, carry):
         for c in range(capacity):
@@ -662,50 +732,29 @@
         return carry
 
     lax.fori_loop(0, devices, pick, 0)
-    for tile in range(slots // LANES):
-        column_ref[tile] = sorted_ref[tile * LANES : (tile + 1) * LANES, :].T
-
+
+    def turn(tile, carry):
+        rows = pl.ds(pl.multiple_of(tile * LANES, LANES), LANES)
+        column_ref[tile] = sorted_ref[rows, :].T
+        return carry
+
+    lax.fori_loop(0, lax.div(size_ref[2] + LANES - 1, LANES), turn, 0)
+
+
+def write_kernel(start_ref, column_ref, place_ref, full_ref, x_ref, r_ref):
     height = 3 * PBLOCK
-    step_width = OUT_TILES * LANES
-
-    def store_copies(n, slot):
-        to = pl.ds(pl.multiple_of(n * step_width, step_width), step_width)
-        return (
-            pltpu.make_async_copy(x_buffer.at[slot], x_ref.at[:, to], x_sem.at[slot]),
-            pltpu.make_async_copy(r_buffer.at[slot], r_ref.at[:, to], r_sem.at[slot]),
-        )
-
-    def write(n, carry):
-        slot = lax.rem(n, 2)
-
-        @pl.when(n >= 2)
-        def _():
-            for copy in store_copies(n - 2, slot):
-                copy.wait()
-
-        for k in range(OUT_TILES):
-            group = n * OUT_TILES + k
-            tile = lax.div(start_smem[group, 0], LANES)
-            index = wide(place_ref[pl.ds(group, 1), :]) & (LANES - 1)
-            split = wide(start_ref[pl.ds(group, 1), :]) & (LANES - 1)
-            present = wide(full_ref[pl.ds(group, 1), :]) > 0.0
-            follow = lane < split
-            for s in range(height // ROWS):
-                for buffer, offset in ((x_buffer, 0), (r_buffer, height)):
-                    rows = slice(offset + s * ROWS, offset + (s + 1) * ROWS)
-                    window = jnp.where(follow, column_ref[tile + 1, rows, :], column_ref[tile, rows, :])
-                    buffer[slot, s * ROWS : (s + 1) * ROWS, k * LANES : (k + 1) * LANES] = jnp.where(
-                        present, lane_take(window, index), 0.0
-                    )
-        for copy in store_copies(n, slot):
-            copy.start()
-        return carry
-
-    steps = groups // OUT_TILES
-    lax.fori_loop(0, steps, write, 0)
-    for n in (steps - 2, steps - 1):
-        for copy in store_copies(n, n % 2):
-            copy.wait()
+    for k in range(OUT_TILES):
+        group = pl.program_id(0) * OUT_TILES + k
+        start = start_ref[group]
+        tile = lax.shift_right_logical(start, 7)
+        index = (wide(place_ref[pl.ds(group, 1), :]) + start) & (LANES - 1)
+        present = wide(full_ref[pl.ds(group, 1), :]) > 0.0
+        for s in range(height // ROWS):
+            for out_ref, offset in ((x_ref, 0), (r_ref, height)):
+                values = column_ref[tile, offset + s * ROWS : offset + (s + 1) * ROWS, :]
+                out_ref[s * ROWS : (s + 1) * ROWS, k * LANES : (k + 1) * LANES] = jnp.where(
+                    present, lane_take(values, index), 0.0
+                )
 
 
 def part_shape(sizes, tod, hit_list, band_lag):
@@ -727,11 +776,12 @@
         and owners == ROWS
         and tiles * ROWS == LANES
         and tiles + 2 + 2 * lag_count <= LANES
-        and reps * tiles % 4 == 0
+        and (wafers, reps) == (2, 2)
+        and reps * tiles % 8 == 0
         and capacity <= LANES
         and devices * capacity % LANES == 0
         and owner_rows % (LANES * OUT_TILES) == 0
-        and 2 * OUT_TILES <= groups <= 2 * LANES
+        and groups <= 2 * LANES
         and 2 * total * total <= BIG
     )
 
@@ -745,58 +795,82 @@
     total = count * ROWS
     slots = devices * capacity
     height = 3 * PBLOCK
+    span = tiles * LANES
+    hit_tiles = tile_limit(shape)
     f32, i32 = jnp.float32, jnp.int32
-    part_axes = ("wafer", "det", "rep")
     vmem, smem = pl.BlockSpec(memory_space=pltpu.VMEM), pl.BlockSpec(memory_space=pltpu.SMEM)
+    anywhere = pl.BlockSpec(memory_space=pl.ANY)
     params = pltpu.CompilerParams(vmem_limit_bytes=VMEM_BYTES)
-    tables = pl.pallas_call(
+    wafer_swap = [(0, 1), (1, 0)]
+
+    def along_det(block):
+        moved = [
+            lax.ppermute(block, "det", [(i, (i + shift) % dets) for i in range(dets)])
+            for shift in range(1, dets)
+        ]
+        return [block] + moved
+
+    def across(blocks_here):
+        here = jnp.stack(blocks_here)
+        other_wafer = lax.ppermute(here, "wafer", wafer_swap)
+        other_rep = lax.ppermute(jnp.stack([here, other_wafer]), "rep", wafer_swap)
+        return here, other_wafer, other_rep
+
+    packed = pl.pallas_call(
         functools.partial(pack_kernel, shape),
-        out_shape=jax.ShapeDtypeStruct((ROWS, 3 * LANES), f32),
-        in_specs=[vmem] * 6,
+        out_shape=jax.ShapeDtypeStruct((ROWS, span + 3 * LANES), f32),
+        in_specs=[vmem] * 7,
         out_specs=vmem,
         compiler_params=params,
         name="pack",
-    )(point_row[0], hit_list[0, 0, 0], group_id, a_zero, band_coef[0].T, band_lag[0].T)
-    tables = lax.all_gather(tables, part_axes, axis=0, tiled=False)
-    angles = lax.all_gather(psi, part_axes, axis=0, tiled=True)
-    samples = lax.all_gather(tod, part_axes, axis=0, tiled=True)
-    own = (lax.axis_index("det") * wafers + lax.axis_index("wafer")).astype(i32).reshape(1)
-    weight, place, full, start, size, pair, group, source, target = pl.pallas_call(
+    )(psi[0], point_row[0], hit_list[0, 0, 0], group_id, a_zero, band_coef[0].T, band_lag[0].T)
+    columns = along_det(packed)
+    samples, *columns = lax.optimization_barrier((tod[0], *columns))
+    angle_blocks = across(columns)
+    sample_blocks = across(along_det(samples))
+    place_here = jnp.stack([lax.axis_index(axis) for axis in ("wafer", "det", "rep")]).astype(i32)
+    weight, place, full, size, pair, group, source, target, start = pl.pallas_call(
         functools.partial(list_kernel, shape),
         out_shape=[
             jax.ShapeDtypeStruct((count, ROWS, LANES), f32),
             jax.ShapeDtypeStruct((2 * LANES, LANES), i32),
             jax.ShapeDtypeStruct((2 * LANES, LANES), f32),
-            jax.ShapeDtypeStruct((2 * LANES, LANES), i32),
-            jax.ShapeDtypeStruct((2,), i32),
+            jax.ShapeDtypeStruct((3,), i32),
             jax.ShapeDtypeStruct((3, total), i32),
             jax.ShapeDtypeStruct((3, total), i32),
             jax.ShapeDtypeStruct((devices, capacity), i32),
             jax.ShapeDtypeStruct((devices, capacity), i32),
+            jax.ShapeDtypeStruct((2 * LANES,), i32),
         ],
-        in_specs=[smem, vmem],
-        out_specs=[vmem] * 4 + [smem] * 5,
+        in_specs=[smem] + [anywhere] * 3,
+        out_specs=[vmem] * 3 + [smem] * 6,
         scratch_shapes=[
+            pltpu.VMEM((devices, ROWS, 3 * LANES), f32),
             pltpu.VMEM((devices, ROWS, LANES), f32),
             pltpu.VMEM((total, 2 * LANES), f32),
             pltpu.VMEM((total, LANES), f32),
             pltpu.VMEM((devices, 2 * ROWS, LANES), i32),
+            pltpu.VMEM((ROWS, 2 * LANES), i32),
             pltpu.SMEM((devices, 2 * ROWS, LANES), i32),
-            pltpu.SemaphoreType.DMA((1,)),
+            pltpu.SMEM((ROWS, 2 * LANES), i32),
+            pltpu.SemaphoreType.DMA((devices,)),
+            pltpu.SemaphoreType.DMA((2,)),
         ],
         compiler_params=params,
         cost_estimate=pl.CostEstimate(flops=10**9, bytes_accessed=4 * 10**6, transcendentals=0),
         name="lists",
-    )(own, tables)
+    )(place_here, *angle_blocks)
     stream = pltpu.VMEM((count, ROWS, LANES), f32)
     sky = pltpu.VMEM((count, 3, ROWS, LANES), f32)
     sky_and_spare = pltpu.VMEM((count + 1, 3, ROWS, LANES), f32)
-    x_turned, r_turned = pl.pallas_call(
+    columns = pl.pallas_call(
         functools.partial(map_kernel, shape),
-        out_shape=[jax.ShapeDtypeStruct((height, owner_rows), f32)] * 2,
-        in_specs=[smem] * 6 + [vmem] * 7,
-        out_specs=[pl.BlockSpec(memory_space=pl.ANY)] * 2,
+        out_shape=jax.ShapeDtypeStruct((hit_tiles, 2 * height, LANES), f32),
+        in_specs=[smem] * 6 + [anywhere] * 6 + [vmem],
+        out_specs=vmem,
         scratch_shapes=[
+            pltpu.VMEM((devices, ROWS, span + LANES), f32),
+            pltpu.VMEM((devices, ROWS, span), f32),
             stream, stream, pltpu.VMEM((teams, blocks + 2, ROWS, LANES), f32), stream,
             sky, sky, sky_and_spare, sky, sky_and_spare,
             pltpu.VMEM((teams, NSUB, ROWS, LANES), f32),
@@ -805,19 +879,23 @@
             pltpu.VMEM((teams, lag_count, ROWS, LANES), f32),
             pltpu.VMEM((teams, lag_count, ROWS, LANES), i32),
             pltpu.VMEM((total, 2 * height), f32),
-            pltpu.VMEM((slots + ROWS, 2 * height), f32),
-            pltpu.VMEM((slots // LANES + 2, 2 * height, LANES), f32),
-            pltpu.VMEM((2, height, OUT_TILES * LANES), f32),
-            pltpu.VMEM((2, height, OUT_TILES * LANES), f32),
-            pltpu.SemaphoreType.DMA((2,)),
-            pltpu.SemaphoreType.DMA((2,)),
+            pltpu.VMEM((hit_tiles * LANES + ROWS, 2 * height), f32),
+            pltpu.SemaphoreType.DMA((devices,)),
+            pltpu.SemaphoreType.DMA((devices,)),
         ],
         compiler_params=params,
         name="map_maker",
-    )(
-        size, pair, group, source, target, start[:, 0:1], tables, angles, samples, weight, place,
-        full, start,
-    )
+    )(place_here, size, pair, group, source, target, *angle_blocks, *sample_blocks, weight)
+    out_block = pl.BlockSpec((height, OUT_TILES * LANES), lambda n: (0, n))
+    x_turned, r_turned = pl.pallas_call(
+        write_kernel,
+        grid=(owner_rows // (OUT_TILES * LANES),),
+        out_shape=[jax.ShapeDtypeStruct((height, owner_rows), f32)] * 2,
+        in_specs=[smem, vmem, vmem, vmem],
+        out_specs=[out_block, out_block],
+        compiler_params=params,
+        name="write",
+    )(start, columns, place, full)
     return x_turned.T, r_turned.T
 
 

time: 215 us -> 162 us (0.75)
  blocking collectives: 25.6 us -> 0 us
  waiting for transfers between devices: 34 us -> 16.7 us
  Pallas kernels: 141 us -> 127 us
  between operations: 14.1 us -> 0.75 us
  starting transfers between devices: 0.08 us -> 12.4 us
  other arithmetic: 0 us -> 2.55 us
    all_gather x2 -> x0, waiting for transfers between devices: 32.6 us -> none  [the longest x1 32.6 us: whole_part(): angles = lax.all_gather(psi, part_axes, axis=0, tiled=True)]
    all_gather x1 -> x0, blocking collectives: 25.6 us -> none  [whole_part(): tables = lax.all_gather(tables, part_axes, axis=0, tiled=False)]
    pallas_call x1 -> x2, Pallas kernels: 118 us -> 101 us  [the longest x1 71.4 us: whole_part(): pl.pallas_call(functools.partial(map_kernel, shape), out_shape=jax.ShapeD...]
    ppermute x0 -> x10, waiting for transfers between devices: none -> 16.7 us  [the longest x6 11 us: along_det(): lax.ppermute(block, 'det', [(i, (i + shift) % dets) for i in range(dets)])]
    ppermute x0 -> x10, starting transfers between devices: none -> 12.4 us  [the longest x6 10.1 us: along_det(): lax.ppermute(block, 'det', [(i, (i + shift) % dets) for i in range(dets)])]
    pallas_call x1, Pallas kernels: 21.7 us -> 24.6 us  [whole_part(): pl.pallas_call(functools.partial(list_kernel, shape), out_shape=[jax.Shap...]
    another operation x0 -> x5, other arithmetic: none -> 2.55 us  [the longest x4 1.89 us: across(): other_rep = lax.ppermute(jnp.stack([here, other_wafer]), 'rep', wafer_swap)]
  transfers between devices with their start and end apart: 2 -> 10, of which waited for: 1 -> 5; matrix products, arithmetic and copies ran while one was open for 0% -> 1% of each run, Pallas kernels for 11% -> 15%
where the time goes in v3:
time: 162 us; the launch traced here: 161 us
  Pallas kernels  127 us (78%)
  waiting for transfers between devices  16.7 us (10%)
  starting transfers between devices  12.4 us (8%)
  other arithmetic  2.55 us (2%)
    pallas_call x1, Pallas kernels, whole_part(): pl.pallas_call(functools.partial(map_kernel, shape), out_shape=jax.ShapeD...  71.4 us
    pallas_call x1, Pallas kernels, whole_part(): pl.pallas_call(write_kernel, grid=(owner_rows // (OUT_TILES * LANES),), o...  29.6 us
    pallas_call x1, Pallas kernels, whole_part(): pl.pallas_call(functools.partial(list_kernel, shape), out_shape=[jax.Shap...  24.6 us
    ppermute x6, waiting for transfers between devices, along_det(): lax.ppermute(block, 'det', [(i, (i + shift) % dets) for i in range(dets)])  11 us
    ppermute x6, starting transfers between devices, along_det(): lax.ppermute(block, 'det', [(i, (i + shift) % dets) for i in range(dets)])  10.1 us
    ppermute x2, waiting for transfers between devices, across(): other_wafer = lax.ppermute(here, 'wafer', wafer_swap)  5.71 us
  transfers between devices with their start and end apart: 10, of which 5 were waited for; matrix products, arithmetic and copies ran while one was open for 1% of the time, Pallas kernels for 15%

profile of v3, /device:TPU:0, one launch (start us, length us, event | category | flops | bytes accessed | tf_op | source)
XLA Modules:
  0.0 161.5 jit_solution(6949004796291345631)
XLA Ops:
  0.6 1.8 %pack.1 = f32[8,2432]{1,0:T(8,128)} custom-call(f32[8,2048]{1,0:T(8,128)} %bitcast.41, s32[8,16]{1,0:T(8,128)} %bitcast.42, s32[8,32]{1,0:T(8,128)} %bitcast.43, s32[1,8]{1,0:T(1,128)} %group_ref.1, f32[1,8]{1,0:T(1,128)} %base_ref.1, f32[4,8]{1,0:T(4,128)} %bitcast.44, s32[4,8]{1,0:T(4,128)} %bitcast.45), custom_call_target="tpu_custom_call" | custom-call | tf_op jit(solution)/shard_map/pack/pallas_call | solution.py:819
  2.5 5.0 %collective-permute-start.2 = (f32[8,2432]{1,0:T(8,128)}, f32[8,2432]{1,0:T(8,128)S(1)}, u32[]{:S(2)}, u32[]{:S(2)}) collective-permute-start(f32[8,2432]{1,0:T(8,128)} %pack.1), channel_id=1, source_target_pairs={{0,12},{4,0},{8,4},{12,8},{1,13},{5,1},{9,5},{13,9},{2,14},{6,2},{... | collective-permute-start | bytes 233480 | tf_op jit(solution)/shard_map/ppermute | solution.py:808
  7.5 1.0 collective-permute-start
  8.5 2.1 %collective-permute-done.2 = f32[8,2432]{1,0:T(8,128)S(1)} collective-permute-done((f32[8,2432]{1,0:T(8,128)}, f32[8,2432]{1,0:T(8,128)S(1)}, u32[]{:S(2)}, u32[]{:S(2)}) %collective-permute-start.2) | collective-permute-done | bytes 77856 | tf_op jit(solution)/shard_map/ppermute | solution.py:808
  10.6 4.3 %collective-permute-done.1 = f32[8,2432]{1,0:T(8,128)S(1)} collective-permute-done((f32[8,2432]{1,0:T(8,128)}, f32[8,2432]{1,0:T(8,128)S(1)}, u32[]{:S(2)}, u32[]{:S(2)}) %collective-permute-start.1) | collective-permute-done | bytes 77856 | tf_op jit(solution)/shard_map/ppermute | solution.py:808
  14.9 0.0 collective-permute-done
  14.9 0.9 fusion.1
  15.9 1.6 collective-permute-start.3
  17.4 2.1 %collective-permute-start.7 = (f32[8,2048]{1,0:T(8,128)}, f32[8,2048]{1,0:T(8,128)S(1)}, u32[]{:S(2)}, u32[]{:S(2)}) collective-permute-start(f32[8,2048]{1,0:T(8,128)} %bitcast.35), channel_id=1, source_target_pairs={{0,12},{4,0},{8,4},{12,8},{1,13},{5,1},{9,5},{13,9},{2,14},{6,2},{... | collective-permute-start | bytes 196616 | tf_op jit(solution)/shard_map/ppermute | solution.py:808
  19.6 2.0 %collective-permute-start.5 = (f32[8,2048]{1,0:T(8,128)}, f32[8,2048]{1,0:T(8,128)S(1)}, u32[]{:S(2)}, u32[]{:S(2)}) collective-permute-start(f32[8,2048]{1,0:T(8,128)} %bitcast.37), channel_id=1, source_target_pairs={{0,4},{4,8},{8,12},{12,0},{1,5},{5,9},{9,13},{13,1},{2,6},{6,10},{... | collective-permute-start | bytes 196616 | tf_op jit(solution)/shard_map/ppermute | solution.py:808
  21.5 0.6 collective-permute-done.7
  22.1 4.0 %collective-permute-done.6 = f32[8,2048]{1,0:T(8,128)S(1)} collective-permute-done((f32[8,2048]{1,0:T(8,128)}, f32[8,2048]{1,0:T(8,128)S(1)}, u32[]{:S(2)}, u32[]{:S(2)}) %collective-permute-start.6) | collective-permute-done | bytes 65568 | tf_op jit(solution)/shard_map/ppermute | solution.py:808
  26.1 0.9 fusion
  27.0 0.6 collective-permute-start.8
  27.6 0.1 collective-permute-start.4
  27.7 5.7 %collective-permute-done.8.tod_across_ref = f32[4,8,2048]{2,1,0:T(8,128)S(1)} collective-permute-done((f32[4,8,2048]{2,1,0:T(8,128)S(1)}, f32[4,8,2048]{2,1,0:T(8,128)S(1)}, u32[]{:S(2)}, u32[]{:S(2)}) %collective-permute-start.8) | collective-permute-done | bytes 262176 | tf_op jit(solution)/shard_map/ppermute | solution.py:815
  33.4 0.1 collective-permute-start.9
  33.5 0.7 pad_add_fusion.self_ref
  34.2 0.0 copy-start.4
  34.2 0.8 copy-done.4
  35.0 24.6 %lists.1 = (f32[256,8,128]{2,1,0:T(8,128)}, s32[256,128]{1,0:T(8,128)}, f32[256,128]{1,0:T(8,128)}, s32[3]{0:T(128)}, s32[3,2048]{1,0:T(4,128)}, /*index=5*/s32[...) custom-call(s32[3]{0:T(128)} %pad_add_fusion.self_ref, f32[4,8,2432]{2,1,0:T(8,128)} %copy-done, ...), custom_call_target="tpu_custom_call" | custom-call | flops 1000000000 | bytes 4000000 | tf_op jit(solution)/shard_map/lists/pallas_call | solution.py:832
  59.7 0.8 copy-done.5
  60.5 71.4 %map_maker.1.column_ref = f32[9,384,128]{2,1,0:T(8,128)} custom-call(s32[3]{0:T(128)} %pad_add_fusion.self_ref, s32[3]{0:T(128)} %get-tuple-element.23.size_ref, s32[3,2048]{1,0:T(4,128)} %get-tuple-element.24.pair_ref, s32[3,2048]{1,0:T(4,128)} %get-tuple-element.25.group_ref, s32[16,32]{1,0:T(8,128)} %get-tuple-element.26.source_ref, ...), custom_call_target="tpu_custom_call" | custom-call | tf_op jit(solution)/shard_map/map_maker/pallas_call | solution.py:866
  131.9 29.6 %write.1 = (f32[192,24576]{1,0:T(8,128)}, f32[192,24576]{1,0:T(8,128)}) custom-call(s32[256]{0:T(256)} %get-tuple-element.22.start_ref, f32[9,384,128]{2,1,0:T(8,128)} %map_maker.1.column_ref, s32[256,128]{1,0:T(8,128)} %get-tuple-element.30.place_ref, f32[256,128]{1,0:T(8,128)} %get-tuple-element.31.full_ref), custom_call_target="tpu_custom_call" | custom-call | tf_op jit(solution)/shard_map/write/pallas_call | solution.py:890
  (17 shorter events, 0.1 us)
Async XLA Ops:
  2.5 8.1 %collective-permute-start.2 = (f32[8,2432]{1,0:T(8,128)}, f32[8,2432]{1,0:T(8,128)S(1)}, u32[]{:S(2)}, u32[]{:S(2)}) collective-permute-start(f32[8,2432]{1,0:T(8,128)} %pack.1), channel_id=1, source_target_pairs={{0,12},{4,0},{8,4},{12,8},{1,13},{5,1},{9,5},{13,9},{2,14},{6,2},{... | collective-permute-start | bytes 233480 | tf_op jit(solution)/shard_map/ppermute | solution.py:808
  7.5 7.4 %collective-permute-start.1 = (f32[8,2432]{1,0:T(8,128)}, f32[8,2432]{1,0:T(8,128)S(1)}, u32[]{:S(2)}, u32[]{:S(2)}) collective-permute-start(f32[8,2432]{1,0:T(8,128)} %pack.1), channel_id=1, source_target_pairs={{0,8},{4,12},{8,0},{12,4},{1,9},{5,13},{9,1},{13,5},{2,10},{6,14},... | collective-permute-start | bytes 233480 | tf_op jit(solution)/shard_map/ppermute | solution.py:808
  7.5 7.4 %collective-permute-start = (f32[8,2432]{1,0:T(8,128)}, f32[8,2432]{1,0:T(8,128)S(1)}, u32[]{:S(2)}, u32[]{:S(2)}) collective-permute-start(f32[8,2432]{1,0:T(8,128)} %pack.1), channel_id=1, source_target_pairs={{0,4},{4,8},{8,12},{12,0},{1,5},{5,9},{9,13},{13,1},{2,6},{6,10},{... | collective-permute-start | bytes 233480 | tf_op jit(solution)/shard_map/ppermute | solution.py:808
  15.9 18.3 %copy-start = (f32[4,8,2432]{2,1,0:T(8,128)}, f32[4,8,2432]{2,1,0:T(8,128)S(1)}, u32[]{:S(2)}) copy-start(f32[4,8,2432]{2,1,0:T(8,128)S(1)} %get-tuple-element.35.here_ref) | copy-start | bytes 933892
  15.9 11.7 %collective-permute-start.3 = (f32[4,8,2432]{2,1,0:T(8,128)S(1)}, f32[4,8,2432]{2,1,0:T(8,128)S(1)}, u32[]{:S(2)}, u32[]{:S(2)}) collective-permute-start(f32[4,8,2432]{2,1,0:T(8,128)S(1)} %get-tuple-element.35.here_ref), channel_id=1, source_target_pairs={{0,2},{2,0},{1,3},{3,1},{4,6},{6,4},{5,7},{7,5},{8,10},{10,8},{9,1... | collective-permute-start | bytes 933896 | tf_op jit(solution)/shard_map/ppermute | solution.py:815
  17.4 4.6 %collective-permute-start.7 = (f32[8,2048]{1,0:T(8,128)}, f32[8,2048]{1,0:T(8,128)S(1)}, u32[]{:S(2)}, u32[]{:S(2)}) collective-permute-start(f32[8,2048]{1,0:T(8,128)} %bitcast.35), channel_id=1, source_target_pairs={{0,12},{4,0},{8,4},{12,8},{1,13},{5,1},{9,5},{13,9},{2,14},{6,2},{... | collective-permute-start | bytes 196616 | tf_op jit(solution)/shard_map/ppermute | solution.py:808
  19.6 6.5 %collective-permute-start.6 = (f32[8,2048]{1,0:T(8,128)}, f32[8,2048]{1,0:T(8,128)S(1)}, u32[]{:S(2)}, u32[]{:S(2)}) collective-permute-start(f32[8,2048]{1,0:T(8,128)} %bitcast.36), channel_id=1, source_target_pairs={{0,8},{4,12},{8,0},{12,4},{1,9},{5,13},{9,1},{13,5},{2,10},{6,14},... | collective-permute-start | bytes 196616 | tf_op jit(solution)/shard_map/ppermute | solution.py:808
  19.6 6.5 %collective-permute-start.5 = (f32[8,2048]{1,0:T(8,128)}, f32[8,2048]{1,0:T(8,128)S(1)}, u32[]{:S(2)}, u32[]{:S(2)}) collective-permute-start(f32[8,2048]{1,0:T(8,128)} %bitcast.37), channel_id=1, source_target_pairs={{0,4},{4,8},{8,12},{12,0},{1,5},{5,9},{9,13},{13,1},{2,6},{6,10},{... | collective-permute-start | bytes 196616 | tf_op jit(solution)/shard_map/ppermute | solution.py:808
  26.9 32.8 %copy-start.2 = (f32[4,8,2048]{2,1,0:T(8,128)}, f32[4,8,2048]{2,1,0:T(8,128)S(1)}, u32[]{:S(2)}) copy-start(f32[4,8,2048]{2,1,0:T(8,128)S(1)} %get-tuple-element.37.tod_here_ref) | copy-start | bytes 786436
  27.0 6.4 %collective-permute-start.8 = (f32[4,8,2048]{2,1,0:T(8,128)S(1)}, f32[4,8,2048]{2,1,0:T(8,128)S(1)}, u32[]{:S(2)}, u32[]{:S(2)}) collective-permute-start(f32[4,8,2048]{2,1,0:T(8,128)S(1)} %get-tuple-element.37.tod_here_ref), channel_id=1, source_target_pairs={{0,2},{2,0},{1,3},{3,1},{4,6},{6,4},{5,7},{7,5},{8,10},{10,8},{9,1... | collective-permute-start | bytes 786440 | tf_op jit(solution)/shard_map/ppermute | solution.py:815
  27.6 6.6 %copy-start.1 = (f32[4,8,2432]{2,1,0:T(8,128)}, f32[4,8,2432]{2,1,0:T(8,128)S(1)}, u32[]{:S(2)}) copy-start(f32[4,8,2432]{2,1,0:T(8,128)S(1)} %collective-permute-done.3.across_ref) | copy-start | bytes 933892
  27.6 6.6 %collective-permute-start.4 = (f32[2,4,8,2432]{3,2,1,0:T(8,128)S(1)}, f32[2,4,8,2432]{3,2,1,0:T(8,128)S(1)}, u32[]{:S(2)}, u32[]{:S(2)}) collective-permute-start(f32[2,4,8,2432]{3,2,1,0:T(8,128)S(1)} %pad_maximum_fusion), channel_id=1, source_target_pairs={{0,1},{1,0},{2,3},{3,2},{4,5},{5,4},{6,7},{7,6},{8,9},{9,8},{10,11... | collective-permute-start | bytes 1867784 | tf_op jit(solution)/shard_map/ppermute | solution.py:816
  33.4 26.3 %copy-start.3 = (f32[4,8,2048]{2,1,0:T(8,128)}, f32[4,8,2048]{2,1,0:T(8,128)S(1)}, u32[]{:S(2)}) copy-start(f32[4,8,2048]{2,1,0:T(8,128)S(1)} %collective-permute-done.8.tod_across_ref) | copy-start | bytes 786436
  33.4 26.2 %collective-permute-start.9 = (f32[2,4,8,2048]{3,2,1,0:T(8,128)S(1)}, f32[2,4,8,2048]{3,2,1,0:T(8,128)S(1)}, u32[]{:S(2)}, u32[]{:S(2)}) collective-permute-start(f32[2,4,8,2048]{3,2,1,0:T(8,128)S(1)} %pad_maximum_fusion.1), channel_id=1, source_target_pairs={{0,1},{1,0},{2,3},{3,2},{4,5},{5,4},{6,7},{7,6},{8,9},{9,8},{10,11... | collective-permute-start | bytes 1572872 | tf_op jit(solution)/shard_map/ppermute | solution.py:816
  34.2 0.8 copy-start.4
  59.7 0.8 copy-start.5
